TPU v7x, 512 devices: a whole 4x4x16 slice. The times are simulated.
512 devices in a mesh: seq: 16 (over z), tensor: 8 (over x, core), dp: 4 (over y).
Axes of the slice: x: 4, y: 4, z: 16, core: 2. Of those that a mesh axis runs over, the one named last changes fastest.
Arguments:
- query_rows: bfloat16 [4, 2048, 8192], P('dp', ('seq', 'tensor')), may hold values from -2 to 2
- key_rows: bfloat16 [4, 2048, 8192], P('dp', ('seq', 'tensor')), may hold values from -2 to 2
- value_rows: bfloat16 [4, 2048, 8192], P('dp', ('seq', 'tensor')), may hold values from -6 to 6
- cotangent: bfloat16 [4, 2048, 8192], P('dp', ('seq', 'tensor')), may hold values from -6 to 6
- norm_gain: float32 [8192], P('tensor'), may hold values from 0.25 to 1.75
- doc_starts: int32 [4, 8], P('dp'), may hold values from 0 to 2047, as said below
Outputs:
- query_grad: bfloat16 [4, 2048, 8192], P('dp', ('seq', 'tensor'))
- key_grad: bfloat16 [4, 2048, 8192], P('dp', ('seq', 'tensor'))
- value_grad: bfloat16 [4, 2048, 8192], P('dp', ('seq', 'tensor'))
- gain_grad: float32 [8192], P('tensor')
Inputs may be any that keep to these rules, and one draw needn't show every extreme that they name: `doc_starts`: each row is strictly increasing, begins with 0 and ends with 2047.
All inputs are finite; a program needn't handle non-finite values.
Results may differ from a plain program's by a relative error of at most 0.0015.
Values may be sent and summed in bfloat16 or wider, within the bound.
A program may use at most 64 MiB of HBM per device.

v0:
```python
import math

import jax
import jax.numpy as jnp
from jax import lax
from jax.sharding import PartitionSpec as P

HEAD_DIM = 128


EPSILON = 1e-05
HIGHEST = lax.Precision.HIGHEST


def carried_in(value, axis, combine, identity, reverse):
    devices, mine = (lax.axis_size(axis), lax.axis_index(axis))
    everything = jax.tree.map(lambda part: lax.all_gather(part, axis), value)
    start = jax.tree.map(
        lambda part, zero: jnp.broadcast_to(jnp.asarray(zero, part.dtype), part.shape),
        value,
        identity,
    )

    def hop(k, before):
        at = devices - 1 - k if reverse else k
        reached = at > mine if reverse else at < mine
        new = combine(before, jax.tree.map(lambda part: part[at], everything))
        return jax.tree.map(lambda a, b: jnp.where(reached, a, b), new, before)

    return lax.fori_loop(0, devices, hop, start)


def segment_of(positions, starts_row):
    return jnp.sum((starts_row[None, :] <= positions[:, None]).astype(jnp.int32), axis=1) - 1


def combine_states(earlier, later):
    return (later[0] + later[1] * earlier[0], earlier[1] * later[1])


def local(query_rows, key_rows, value_rows, cotangent, norm_gain, doc_starts):
    query_all, key_all, value_all, cot_all = (
        lax.all_to_all(query_rows, "tensor", split_axis=2, concat_axis=1, tiled=True),
        lax.all_to_all(key_rows, "tensor", split_axis=2, concat_axis=1, tiled=True),
        lax.all_to_all(value_rows, "tensor", split_axis=2, concat_axis=1, tiled=True),
        lax.all_to_all(cotangent, "tensor", split_axis=2, concat_axis=1, tiled=True),
    )
    block_len = query_all.shape[1]
    local_width = query_all.shape[2]
    heads_dev = local_width // HEAD_DIM
    query_loc = query_all.reshape(block_len, heads_dev, HEAD_DIM)
    key_loc = key_all.reshape(block_len, heads_dev, HEAD_DIM)
    value_loc = value_all.reshape(block_len, heads_dev, HEAD_DIM)
    seq_index = lax.axis_index("seq")
    first_row = seq_index * block_len
    row_ids = jnp.arange(block_len, dtype=jnp.int32)
    starts_row = doc_starts[0]
    segment = segment_of(first_row + row_ids, starts_row)
    before_seg = segment_of(jnp.reshape(first_row - 1, (1,)), starts_row)[0]
    prev_seg = jnp.where(seq_index > 0, before_seg, -1)
    last_seg = segment[-1]
    causal = row_ids[:, None] >= row_ids[None, :]
    doc_mask = (causal & (segment[:, None] == segment[None, :])).astype(jnp.float32)
    uses_state = (segment == prev_seg).astype(jnp.float32)
    keep_flag = segment == last_seg
    keep_key = keep_flag.astype(jnp.float32)
    carry_flag = (prev_seg == last_seg).astype(jnp.float32)
    query_f = query_loc.astype(jnp.float32)
    key_f = key_loc.astype(jnp.float32)
    value_f = value_loc.astype(jnp.float32)
    local_state = jnp.einsum(
        "sha,shb->hab",
        key_loc * keep_flag.astype(jnp.bfloat16)[:, None, None],
        value_loc,
        preferred_element_type=jnp.float32,
    )
    zero_state = jnp.zeros(local_state.shape, jnp.float32)
    state_in, flag_prefix = carried_in(
        (local_state, carry_flag), "seq", combine_states, (zero_state, jnp.float32(1.0)), False
    )
    scores = jnp.einsum("tha,sha->hts", query_loc, key_loc, preferred_element_type=jnp.float32)
    masked = scores * doc_mask[None]
    attended = jnp.einsum("hts,shb->thb", masked, value_f, precision=HIGHEST)
    attended = attended + uses_state[:, None, None] * jnp.einsum(
        "tha,hab->thb", query_f, state_in, precision=HIGHEST
    )
    centre = jnp.mean(attended, axis=-1, keepdims=True)
    centered = attended - centre
    spread = jnp.mean(centered * centered, axis=-1, keepdims=True)
    inv_std = lax.rsqrt(spread + EPSILON)
    normed = centered * inv_std
    gain_loc = norm_gain.reshape(heads_dev, HEAD_DIM)
    upstream = cot_all.reshape(block_len, heads_dev, HEAD_DIM).astype(jnp.float32)
    gain_part = jnp.sum(upstream * normed, axis=0)
    d_normed = upstream * gain_loc[None]
    d_att = inv_std * (
        d_normed
        - jnp.mean(d_normed, axis=-1, keepdims=True)
        - normed * jnp.mean(d_normed * normed, axis=-1, keepdims=True)
    )
    d_scores = jnp.einsum("thb,shb->hts", d_att, value_f, precision=HIGHEST) * doc_mask[None]
    state_grad = jnp.einsum(
        "tha,thb->hab", query_f, uses_state[:, None, None] * d_att, precision=HIGHEST
    )
    out_grad, grad_flag = carried_in(
        (state_grad, carry_flag), "seq", combine_states, (zero_state, jnp.float32(1.0)), True
    )
    d_query = jnp.einsum("hts,sha->tha", d_scores, key_f, precision=HIGHEST)
    d_query = d_query + uses_state[:, None, None] * jnp.einsum(
        "thb,hab->tha", d_att, state_in, precision=HIGHEST
    )
    d_key = jnp.einsum("hts,tha->sha", d_scores, query_f, precision=HIGHEST)
    d_key = d_key + keep_key[:, None, None] * jnp.einsum(
        "shb,hab->sha", value_f, out_grad, precision=HIGHEST
    )
    d_value = jnp.einsum("hts,thb->shb", masked, d_att, precision=HIGHEST)
    d_value = d_value + keep_key[:, None, None] * jnp.einsum(
        "sha,hab->shb", key_f, out_grad, precision=HIGHEST
    )
    out_shape = (1, block_len, local_width)
    grad_query, grad_key, grad_value = (
        lax.all_to_all(
            d_query.astype(jnp.bfloat16).reshape(out_shape),
            "tensor",
            split_axis=1,
            concat_axis=2,
            tiled=True,
        ),
        lax.all_to_all(
            d_key.astype(jnp.bfloat16).reshape(out_shape),
            "tensor",
            split_axis=1,
            concat_axis=2,
            tiled=True,
        ),
        lax.all_to_all(
            d_value.astype(jnp.bfloat16).reshape(out_shape),
            "tensor",
            split_axis=1,
            concat_axis=2,
            tiled=True,
        ),
    )
    total_tokens = lax.axis_size("dp") * lax.axis_size("seq") * block_len
    gain_total = lax.psum(gain_part.reshape(local_width), ("seq", "dp"))
    gain_grad = gain_total / math.sqrt(total_tokens)
    return (grad_query, grad_key, grad_value, gain_grad)


def solution(mesh):
    return jax.shard_map(
        local,
        mesh=mesh,
        in_specs=(
            P("dp", ("seq", "tensor"), None),
            P("dp", ("seq", "tensor"), None),
            P("dp", ("seq", "tensor"), None),
            P("dp", ("seq", "tensor"), None),
            P("tensor"),
            P("dp", None),
        ),
        out_specs=(
            P("dp", ("seq", "tensor"), None),
            P("dp", ("seq", "tensor"), None),
            P("dp", ("seq", "tensor"), None),
            P("tensor"),
        ),
        check_vma=False,
    )
```

profile of v0, /device:TPU:4, one launch (start us, length us, event | category | flops | bytes accessed | tf_op | source)
XLA Modules:
  0.0 717.4 jit_solution(5263217792780141048)
XLA Ops:
  7.2 8.3 %copy.153 = bf16[1,16,8192]{1,0,2:T(2,128)(2,1)} copy(bf16[1,16,8192]{2,1,0:T(8,128)(2,1)} %param.11) | data formatting | bytes 524288 | tf_op args[1]
  16.0 45.3 %reduce.2 = bf16[8192,16]{1,0:T(8,128)(2,1)S(1)} reduce(bf16[8192,1,16]{2,1,0:T(2,128)(2,1)} %bitcast.139, bf16[]{:T(256)} %broadcast.128), dimensions={1}, to_apply=%bitcast.104.reduce_sub_computation | reduce | bytes 524290
  64.1 9.8 %all-to-all-start.1 = ((bf16[8,2,8192]{2,1,0:T(2,128)(2,1)}), bf16[8,2,8192]{2,1,0:T(2,128)(2,1)S(1)}, u32[]{:S(2)}, u32[]{:S(2)}) async-start(bf16[8,2,8192]{2,1,0:T(2,128)(2,1)} %reshape.152), calls=%async_computation.1 | async-start | bytes 524288 | tf_op jit(solution)/shard_map/all_to_all | solution.py:44
  75.9 6.7 copy.158
  82.6 45.2 %reduce.3 = bf16[8192,16]{1,0:T(8,128)(2,1)S(1)} reduce(bf16[8192,1,16]{2,1,0:T(2,128)(2,1)} %bitcast.144, bf16[]{:T(256)} %broadcast.128), dimensions={1}, to_apply=%bitcast.106.reduce_sub_computation | reduce | bytes 524290
  136.3 5.1 reshape.153
  141.4 7.9 %copy.154 = bf16[1,16,8192]{2,1,0:T(8,128)(2,1)S(1)} copy(bf16[1,16,8192]{1,0,2:T(2,128)(2,1)} %bitcast.140) | data formatting | bytes 524288 | tf_op jit(solution)/shard_map/all_to_all | solution.py:44
  149.6 5.1 reshape.155
  154.8 7.9 %copy.159 = bf16[1,16,8192]{2,1,0:T(8,128)(2,1)S(1)} copy(bf16[1,16,8192]{1,0,2:T(2,128)(2,1)} %bitcast.141) | data formatting | bytes 524288 | tf_op jit(solution)/shard_map/all_to_all | solution.py:45
  164.4 6.8 copy.150
  171.1 45.3 %reduce.4 = bf16[8192,16]{1,0:T(8,128)(2,1)S(1)} reduce(bf16[8192,1,16]{2,1,0:T(2,128)(2,1)} %bitcast.145, bf16[]{:T(256)} %broadcast.128), dimensions={1}, to_apply=%bitcast.108.reduce_sub_computation | reduce | bytes 524290
  225.0 6.8 copy.166
  231.7 45.2 %reduce.1 = bf16[8192,16]{1,0:T(8,128)(2,1)S(1)} reduce(bf16[8192,1,16]{2,1,0:T(2,128)(2,1)} %bitcast.146, bf16[]{:T(256)} %broadcast.128), dimensions={1}, to_apply=%bitcast.102.reduce_sub_computation | reduce | bytes 524290
  281.9 32.1 %all-reduce = f32[16]{0:T(128)S(1)} all-reduce(f32[16]{0:T(128)S(1)} %dynamic-update-slice), channel_id=1, replica_groups=mesh['seq'=16,'tensor'=8,'dp'=4] {'seq'}, use_global_device_ids=true, to_apply=%add | all-reduce | flops 16 | bytes 128
  319.2 5.1 reshape.157
  324.3 7.9 %copy.151 = bf16[1,16,8192]{2,1,0:T(8,128)(2,1)S(1)} copy(bf16[1,16,8192]{1,0,2:T(2,128)(2,1)} %bitcast.142) | data formatting | bytes 524288 | tf_op jit(solution)/shard_map/all_to_all | solution.py:43
  332.6 5.1 reshape.151
  337.7 8.5 %bitcast_convert_fusion = f32[1,16,8192]{1,0,2:T(1,128)} fusion(bf16[8192,1,16]{2,1,0:T(2,128)(2,1)} %reshape.151), kind=kLoop, calls=%fused_computation.66 | loop fusion | flops 131072 | bytes 786432 | tf_op jit(solution)/shard_map/convert_element_type | solution.py:93
  349.7 43.6 %while.30 = (s32[]{:T(128)}, f32[8,128,128]{2,1,0:T(8,128)S(1)}, s32[]{:T(128)}, f32[16,8,128,128]{3,2,1,0:T(8,128)}, f32[16]{0:T(128)S(1)}, /*index=5*/s32[]{:T(128)}, s32[]{:T(128)}) while((s32[]{:T(128)}, f32[8,128,128]{2,1,0:T(8,128)S(1)}, s32[]{:T(128)}, f32[16,8,128,128]{3,2,1,0:T(8,128)}, f32[16]{0:T(128)S(1)}, ...), condition=%wide.region_3.4_spmd.clone, body=%wide.region_2.3_spmd.clone.sunk | while | flops 524292 | bytes 1572981 | solution.py:30
  404.2 5.1 all-to-all-start.4
  409.3 90.6 %all-gather.7.cloned.1.call-done = f32[128,128,128]{2,1,0:T(8,128)} async-done(((f32[8,128,128]{2,1,0:T(8,128)}), f32[128,128,128]{2,1,0:T(8,128)}) %all-gather.7.cloned.1.call-update) | async-done | bytes 8388624 | tf_op jit(solution)/shard_map/all_gather | solution.py:17
  499.9 43.7 %while.31 = (s32[]{:T(128)}, f32[8,128,128]{2,1,0:T(8,128)S(1)}, s32[]{:T(128)}, f32[16,8,128,128]{3,2,1,0:T(8,128)}, f32[16]{0:T(128)S(1)}, /*index=5*/s32[]{:T(128)}, s32[]{:T(128)}, s32[]{:T(128)}, s32[]{:T(128)}) while((s32[]{:T(128)}, f32[8,128,128]{2,1,0:T(8,128)S(1)}, s32[]{:T(128)}, f32[16,8,128,128]{3,2,1,0:T(8,128)}, ...), condition=%wide.region_9.10_spmd.clone, body=%wide.region_8.9_spmd.clone.sunk | while | flops 524296 | bytes 1573043 | solution.py:30
  558.3 6.5 all-to-all-start.5
  564.8 141.5 %psum.7 = f32[1024]{0:T(1024)S(1)} all-reduce(f32[1024]{0:T(1024)S(1)} %bitcast.188), channel_id=1, replica_groups=mesh['seq'=16,'tensor'=8,'dp'=4] {'seq','dp'}, use_global_device_ids=true, to_apply=%region_11.12 | all-reduce | flops 1024 | bytes 8192 | tf_op jit(solution)/shard_map/psum | solution.py:145
  (167 shorter events, 152.8 us)
Async XLA Ops:
  16.0 57.9 %copy-start.7 = (s32[1,8]{1,0:T(1,128)S(1)}, s32[1,8]{1,0:T(1,128)}, u32[]{:S(2)}) copy-start(s32[1,8]{1,0:T(1,128)} %param.15) | copy-start | bytes 100
  16.0 59.9 %copy-start.3 = (bf16[1,16,8192]{2,1,0:T(8,128)(2,1)S(1)}, bf16[1,16,8192]{2,1,0:T(8,128)(2,1)}, u32[]{:S(2)}) copy-start(bf16[1,16,8192]{2,1,0:T(8,128)(2,1)} %param.12) | copy-start | bytes 786436
  64.1 67.2 %all-to-all-start.1 = ((bf16[8,2,8192]{2,1,0:T(2,128)(2,1)}), bf16[8,2,8192]{2,1,0:T(2,128)(2,1)S(1)}, u32[]{:S(2)}, u32[]{:S(2)}) async-start(bf16[8,2,8192]{2,1,0:T(2,128)(2,1)} %reshape.152), calls=%async_computation.1 | async-start | bytes 524288 | tf_op jit(solution)/shard_map/all_to_all | solution.py:44
  131.3 18.4 %all-to-all-start.2 = ((bf16[8,2,8192]{2,1,0:T(2,128)(2,1)}), bf16[8,2,8192]{2,1,0:T(2,128)(2,1)S(1)}, u32[]{:S(2)}, u32[]{:S(2)}) async-start(bf16[8,2,8192]{2,1,0:T(2,128)(2,1)} %reshape.154), calls=%async_computation.2 | async-start | bytes 524288 | tf_op jit(solution)/shard_map/all_to_all | solution.py:45
  136.1 213.5 %all-gather.5.cloned.1.call-start = ((), (), s32[]{:S(2)}) async-start(), calls=%async_computation.7 | async-start | bytes 8912896 | tf_op jit(solution)/shard_map/all_gather | solution.py:17
  154.8 9.6 %copy-start.4 = (bf16[1,16,8192]{2,1,0:T(8,128)(2,1)S(1)}, bf16[1,16,8192]{2,1,0:T(8,128)(2,1)}, u32[]{:S(2)}) copy-start(bf16[1,16,8192]{2,1,0:T(8,128)(2,1)} %param.10) | copy-start | bytes 786436
  171.1 53.8 %copy-start.5 = (bf16[1,16,8192]{2,1,0:T(8,128)(2,1)S(1)}, bf16[1,16,8192]{2,1,0:T(8,128)(2,1)}, u32[]{:S(2)}) copy-start(bf16[1,16,8192]{2,1,0:T(8,128)(2,1)} %param.13) | copy-start | bytes 786436
  219.2 94.9 %all-to-all-start = ((bf16[8,2,8192]{2,1,0:T(2,128)(2,1)}), bf16[8,2,8192]{2,1,0:T(2,128)(2,1)S(1)}, u32[]{:S(2)}, u32[]{:S(2)}) async-start(bf16[8,2,8192]{2,1,0:T(2,128)(2,1)} %reshape.156), calls=%async_computation | async-start | bytes 524288 | tf_op jit(solution)/shard_map/all_to_all | solution.py:43
  314.1 18.5 %all-to-all-start.3 = ((bf16[8,2,8192]{2,1,0:T(2,128)(2,1)}), bf16[8,2,8192]{2,1,0:T(2,128)(2,1)S(1)}, u32[]{:S(2)}, u32[]{:S(2)}) async-start(bf16[8,2,8192]{2,1,0:T(2,128)(2,1)} %reshape.150), calls=%async_computation.3 | async-start | bytes 524288 | tf_op jit(solution)/shard_map/all_to_all | solution.py:46
  318.9 181.0 %all-gather.7.cloned.1.call-start = ((), (), s32[]{:S(2)}) async-start(), calls=%async_computation.8 | async-start | bytes 8912896 | tf_op jit(solution)/shard_map/all_gather | solution.py:17
  349.3 45.4 %copy-start.2 = (f32[128,8,128]{0,2,1:T(8,128)}, f32[128,8,128]{0,2,1:T(8,128)S(1)}, u32[]{:S(2)}) copy-start(f32[128,8,128]{0,2,1:T(8,128)S(1)} %copy.168) | copy-start | bytes 1572868
  349.7 45.0 %copy-start.6 = (f32[1024]{0:T(1024)S(1)}, f32[1024]{0:T(1024)}, u32[]{:S(2)}) copy-start(f32[1024]{0:T(1024)} %param.14) | copy-start | bytes 12292
  398.5 0.8 copy-start
  404.2 144.9 %all-to-all-start.4 = ((bf16[8,2,8192]{2,1,0:T(2,128)(2,1)}), bf16[8,2,8192]{2,1,0:T(2,128)(2,1)S(1)}, u32[]{:S(2)}, u32[]{:S(2)}) async-start(bf16[8,2,8192]{2,1,0:T(2,128)(2,1)} %reshape.158), calls=%async_computation.4 | async-start | bytes 524288 | tf_op jit(solution)/shard_map/all_to_all | solution.py:122
  543.6 10.3 %copy-start.1 = (f32[8,128,128]{2,1,0:T(8,128)S(1)}, f32[8,128,128]{2,1,0:T(8,128)}, u32[]{:S(2)}) copy-start(f32[8,128,128]{2,1,0:T(8,128)} %copy-done) | copy-start | bytes 1572868
  549.1 9.2 %all-to-all-start.6 = ((bf16[8,2,8192]{2,1,0:T(2,128)(2,1)}), bf16[8,2,8192]{2,1,0:T(2,128)(2,1)S(1)}, u32[]{:S(2)}, u32[]{:S(2)}) async-start(bf16[8,2,8192]{2,1,0:T(2,128)(2,1)} %reshape.162), calls=%async_computation.6 | async-start | bytes 524288 | tf_op jit(solution)/shard_map/all_to_all | solution.py:136
  558.3 150.8 %all-to-all-start.5 = ((bf16[8,2,8192]{2,1,0:T(2,128)(2,1)}), bf16[8,2,8192]{2,1,0:T(2,128)(2,1)S(1)}, u32[]{:S(2)}, u32[]{:S(2)}) async-start(bf16[8,2,8192]{2,1,0:T(2,128)(2,1)} %reshape.160), calls=%async_computation.5 | async-start | bytes 524288 | tf_op jit(solution)/shard_map/all_to_all | solution.py:129
Sparse Core Ops, SparseCore 0:
  164.5 105.9 all-gather.4
  398.0 101.8 all-gather.6
where the time goes:
time: 727 us; the launch traced here: 717 us
  other arithmetic  268 us (37%)
  blocking collectives  174 us (24%)
  local copies, waits for them, and re-layouts  119 us (16%)
  waiting for transfers between devices  91 us (13%)
  starting transfers between devices  41.3 us (6%)
  between operations  16.4 us (2%)
  matrix products  7.34 us (1%)
    unnamed x9, other arithmetic  187 us
    psum x1, blocking collectives, local(): gain_total = lax.psum(gain_part.reshape(local_width), ('seq', 'dp'))  141 us
    all_gather x2, waiting for transfers between devices, carried_in(): everything = jax.tree.map(lambda part: lax.all_gather(part, axis), value)  90.6 us
    unnamed x48, local copies, waits for them, and re-layouts  68.2 us
    select_n x32, other arithmetic, hop(): return jax.tree.map(lambda a, b: jnp.where(reached, a, b), new, before)  67.9 us
    unnamed x1, blocking collectives  32.1 us
    dynamic_slice x32, local copies, waits for them, and re-layouts, hop(): new = combine(before, jax.tree.map(lambda part: part[at], everything))  18.8 us
  transfers between devices with their start and end apart: 9, of which 2 were waited for; matrix products, arithmetic and copies ran while one was open for 38% of the time, Pallas kernels for 0%

commit v1 on v0

v1 whole, which is shorter than its diff:
```python
import functools
import math

import jax
import jax.numpy as jnp
from jax import lax
from jax.experimental import pallas as pl
from jax.experimental.pallas import tpu as pltpu
from jax.sharding import PartitionSpec as P

MESH = pl.DeviceIdType.MESH
F32 = jnp.float32
BF16 = jnp.bfloat16
EPSILON = 1e-05
DIM = 128
HEADS = 4
TOK = 256
COLS = HEADS * DIM
ROWS = 16
GROUP = 16
SEQ = 16
PAIRS = 8
SUB = 4
PIECE = DIM // SUB
NC = HEADS * SUB


def split(x):
    hi = x.astype(BF16)
    return hi, (x - hi.astype(F32)).astype(BF16)


def mm(a, b, ca=1, cb=0):
    return lax.dot_general(a, b, (((ca,), (cb,)), ((), ())), preferred_element_type=F32)


def kernel(
    k_ref, v_ref, q_ref, c_ref, gain_ref, starts_ref,
    out_ref, gout_ref,
    buf, mask, use, keep, own, frecv, fsend, brecv, bsend, scores, dh, dl, dkl, dvl, obuf,
    gsrc, gy, gz,
    in_send, in_recv, f_send, f_recv, b_send, b_recv, o_send, o_recv,
    gy_send, gy_recv, gz_send, gz_recv,
):
    z, t, y = lax.axis_index("seq"), lax.axis_index("tensor"), lax.axis_index("dp")
    p, j = z // 2, lax.rem(z, 2)
    base = p * 2
    me = j * 8 + t
    after, before = lax.rem(z + 2, SEQ), lax.rem(z + SEQ - 2, SEQ)

    def peer(s):
        g = lax.rem(me + s, GROUP)
        return g, g // 8, lax.rem(g, 8)

    barrier = pltpu.get_barrier_semaphore()

    def greet(zz, tt, yy):
        pl.semaphore_signal(barrier, inc=1, device_id=(zz, tt, yy), device_id_type=MESH)

    def greet_group(s, _):
        _, jj, tt = peer(s)
        greet(base + jj, tt, y)
        return 0

    lax.fori_loop(1, GROUP, greet_group, 0)

    def greet_seq(s, _):
        zz = lax.rem(base + s, SEQ)
        greet(zz, t, y)
        return 0

    lax.fori_loop(2, SEQ, greet_seq, 0)
    for s in range(1, 4):
        greet(z, t, lax.rem(y + s, 4))
    pl.semaphore_wait(barrier, 15 + 14 + 3)

    def send_in(refs):
        def body(s, _):
            _, jj, tt = peer(s)
            col = pl.multiple_of(tt * 1024 + jj * COLS, DIM)
            for a, ref in refs:
                pltpu.make_async_remote_copy(
                    src_ref=ref.at[0, :, pl.ds(col, COLS)],
                    dst_ref=buf.at[a, pl.ds(pl.multiple_of(me * ROWS, ROWS), ROWS), :],
                    send_sem=in_send.at[a],
                    recv_sem=in_recv.at[a],
                    device_id=(base + jj, tt, y),
                    device_id_type=MESH,
                ).start()
            return 0

        lax.fori_loop(1, GROUP, body, 0)
        for a, ref in refs:
            pltpu.make_async_copy(
                ref.at[0, :, pl.ds(pl.multiple_of(t * 1024 + j * COLS, DIM), COLS)],
                buf.at[a, pl.ds(pl.multiple_of(me * ROWS, ROWS), ROWS), :],
                in_recv.at[a],
            ).start()

    def wait_in(a):
        pltpu.make_async_copy(buf.at[a], buf.at[a], in_recv.at[a]).wait()

    send_in(((0, k_ref), (1, v_ref)))
    send_in(((2, q_ref), (3, c_ref)))

    def count(tok):
        total = jnp.zeros_like(tok)
        for i in range(8):
            total = total + (starts_ref[0, i] <= tok).astype(jnp.int32)
        return total

    first = base * 128
    prev = count(first - 1)
    last = count(first + TOK - 1)
    carry = (prev == last).astype(F32)
    row = lax.broadcasted_iota(jnp.int32, (TOK, DIM), 0) + first
    seg = count(row)
    use[...] = (seg == prev).astype(F32)
    keep[...] = (seg == last).astype(F32)
    seg_row = count(lax.broadcasted_iota(jnp.int32, (8, TOK), 1) + first)[:1]
    seg_col = jnp.concatenate([seg, seg], axis=1)
    rows = lax.broadcasted_iota(jnp.int32, (TOK, TOK), 0)
    cols = lax.broadcasted_iota(jnp.int32, (TOK, TOK), 1)
    mask[...] = ((rows >= cols) & (seg_col == seg_row)).astype(F32)
    gsrc[...] = jnp.zeros_like(gsrc)

    @pl.when(p == 0)
    def _():
        frecv[...] = jnp.zeros_like(frecv)

    @pl.when(p == PAIRS - 1)
    def _():
        brecv[...] = jnp.zeros_like(brecv)

    def take(a, h):
        return buf[a, :, pl.ds(pl.multiple_of(h * DIM, DIM), DIM)]

    wait_in(0)
    wait_in(1)

    def local_state(h, _):
        kept = take(0, h) * keep[...].astype(BF16)
        own[h] = mm(kept, take(1, h), 0, 0)
        return 0

    lax.fori_loop(0, HEADS, local_state, 0)

    def piece(ref, c):
        return ref.at[c // SUB, pl.ds(pl.multiple_of(lax.rem(c, SUB) * PIECE, PIECE), PIECE), :]

    def fcopy(c):
        return pltpu.make_async_remote_copy(
            src_ref=piece(fsend, c), dst_ref=piece(frecv, c),
            send_sem=f_send.at[c], recv_sem=f_recv.at[c],
            device_id=(after, t, y), device_id_type=MESH,
        )

    def bcopy(c):
        return pltpu.make_async_remote_copy(
            src_ref=piece(bsend, c), dst_ref=piece(brecv, c),
            send_sem=b_send.at[c], recv_sem=b_recv.at[c],
            device_id=(before, t, y), device_id_type=MESH,
        )

    def forward(c, _):
        @pl.when(p > 0)
        def _():
            fcopy(c).wait_recv()

        @pl.when(p < PAIRS - 1)
        def _():
            piece(fsend, c)[...] = piece(own, c)[...] + carry * piece(frecv, c)[...]
            fcopy(c).start()

        return 0

    def local_scores(h, _):
        scores[h] = mm(take(2, h), take(0, h), 1, 1) * mask[...]
        return 0

    def first_half(s, _):
        @pl.when((s == 0) == (p < PAIRS // 2))
        def _():
            lax.fori_loop(0, NC, forward, 0)

        @pl.when((s == 0) != (p < PAIRS // 2))
        def _():
            wait_in(2)
            lax.fori_loop(0, HEADS, local_scores, 0)

        return 0

    lax.fori_loop(0, 2, first_half, 0)
    wait_in(3)

    def attend(h, _):
        query, value = take(2, h), take(1, h)
        sh, sl = split(scores[h])
        th, tl = split(frecv[h])
        att = mm(sh, value) + mm(sl, value) + use[...] * (mm(query, th) + mm(query, tl))
        centered = att - jnp.mean(att, axis=-1, keepdims=True)
        inv = lax.rsqrt(jnp.mean(centered * centered, axis=-1, keepdims=True) + EPSILON)
        normed = centered * inv
        up = take(3, h).astype(F32)
        at = j * HEADS + h
        gsrc[pl.ds(at, 1), :] = jnp.sum(up * normed, axis=0, keepdims=True)
        dn = up * gain_ref[pl.ds(at, 1), :]
        d_att = inv * (
            dn
            - jnp.mean(dn, axis=-1, keepdims=True)
            - normed * jnp.mean(dn * normed, axis=-1, keepdims=True)
        )
        hi, lo = split(d_att)
        dh[h] = hi
        dl[h] = lo
        used = use[...].astype(BF16)
        bsend[h] = mm(query, hi * used, 0, 0) + mm(query, lo * used, 0, 0)

        @pl.when(p == PAIRS - 1)
        def _():
            for s in range(SUB):
                bcopy(h * SUB + s).start()

        return 0

    lax.fori_loop(0, HEADS, attend, 0)

    gy[y] = gsrc[...]

    def gy_copy(yy):
        return pltpu.make_async_remote_copy(
            src_ref=gy.at[y], dst_ref=gy.at[y], send_sem=gy_send.at[yy], recv_sem=gy_recv.at[y],
            device_id=(z, t, yy), device_id_type=MESH,
        )

    for s in range(1, 4):
        gy_copy(lax.rem(y + s, 4)).start()

    def backward(c, _):
        @pl.when(p < PAIRS - 1)
        def _():
            bcopy(c).wait_recv()

            @pl.when(p > 0)
            def _():
                piece(bsend, c)[...] += carry * piece(brecv, c)[...]
                bcopy(c).start()

        return 0

    def send_out(i):
        def body(s, _):
            g, jj, tt = peer(s)
            pltpu.make_async_remote_copy(
                src_ref=obuf.at[i, pl.ds(pl.multiple_of(g * ROWS, ROWS), ROWS), :],
                dst_ref=out_ref.at[i, :, pl.ds(pl.multiple_of(t * 1024 + j * COLS, DIM), COLS)],
                send_sem=o_send.at[i],
                recv_sem=o_recv.at[i],
                device_id=(base + jj, tt, y),
                device_id_type=MESH,
            ).start()
            return 0

        lax.fori_loop(1, GROUP, body, 0)
        pltpu.make_async_copy(
            obuf.at[i, pl.ds(pl.multiple_of(me * ROWS, ROWS), ROWS), :],
            out_ref.at[i, :, pl.ds(pl.multiple_of(t * 1024 + j * COLS, DIM), COLS)],
            o_recv.at[i],
        ).start()

    def put(i, h, value):
        obuf[i, :, pl.ds(pl.multiple_of(h * DIM, DIM), DIM)] = value.astype(BF16)

    def local_grads(h, _):
        key, value, query = take(0, h), take(1, h), take(2, h)
        hi, lo = dh[h], dl[h]
        d_sc = (mm(hi, value, 1, 1) + mm(lo, value, 1, 1)) * mask[...]
        eh, el = split(d_sc)
        th, tl = split(frecv[h])
        sh, sl = split(scores[h])
        d_query = mm(eh, key) + mm(el, key)
        d_query = d_query + use[...] * (mm(hi, th, 1, 1) + mm(hi, tl, 1, 1) + mm(lo, th, 1, 1))
        put(0, h, d_query)
        dkl[h] = mm(eh, query, 0, 0) + mm(el, query, 0, 0)
        dvl[h] = mm(sh, hi, 0, 0) + mm(sl, hi, 0, 0) + mm(sh, lo, 0, 0)
        return 0

    def second_half(s, _):
        @pl.when((s == 0) == (p >= PAIRS // 2))
        def _():
            lax.fori_loop(0, NC, backward, 0)

        @pl.when((s == 0) != (p >= PAIRS // 2))
        def _():
            lax.fori_loop(0, HEADS, local_grads, 0)
            send_out(0)

        return 0

    lax.fori_loop(0, 2, second_half, 0)

    for s in range(1, 4):
        yy = lax.rem(y + s, 4)
        pltpu.make_async_copy(gy.at[yy], gy.at[yy], gy_recv.at[yy]).wait()
    gz[z] = (gy[0] + gy[1]) + (gy[2] + gy[3])

    def gz_start(s, _):
        pltpu.make_async_remote_copy(
            src_ref=gz.at[z], dst_ref=gz.at[z], send_sem=gz_send, recv_sem=gz_recv,
            device_id=(lax.rem(z + s, SEQ), t, y), device_id_type=MESH,
        ).start()
        return 0

    def last_grads(h, _):
        key, value = take(0, h), take(1, h)
        gh, gl = split(brecv[h])
        put(1, h, dkl[h] + keep[...] * (mm(value, gh, 1, 1) + mm(value, gl, 1, 1)))
        put(2, h, dvl[h] + keep[...] * (mm(key, gh) + mm(key, gl)))
        return 0

    lax.fori_loop(0, HEADS, last_grads, 0)
    send_out(1)
    send_out(2)
    lax.fori_loop(1, SEQ, gz_start, 0)

    part = gz.at[pl.ds(0, SEQ - 1)]
    pltpu.make_async_copy(part, part, gz_recv).wait()
    total = gz[0]
    for s in range(1, SEQ):
        total = total + gz[s]
    gout_ref[...] = total / math.sqrt(4 * SEQ * 128)

    for i in range(3):
        pltpu.make_async_copy(out_ref.at[i], out_ref.at[i], o_recv.at[i]).wait()
    for a in range(4):
        part = buf.at[a, pl.ds(0, TOK - ROWS), :]
        pltpu.make_async_copy(part, part, in_send.at[a]).wait()
    for i in range(3):
        part = obuf.at[i, pl.ds(0, TOK - ROWS), :]
        pltpu.make_async_copy(part, part, o_send.at[i]).wait()
    part = gz.at[pl.ds(0, SEQ - 1)]
    pltpu.make_async_copy(part, part, gz_send).wait()
    for s in range(1, 4):
        gy_copy(lax.rem(y + s, 4)).wait_send()

    def drain(c, _):
        @pl.when(p < PAIRS - 1)
        def _():
            fcopy(c).wait_send()

        @pl.when(p > 0)
        def _():
            bcopy(c).wait_send()

        return 0

    lax.fori_loop(0, NC, drain, 0)


def place(grads_ref, gain_ref, q_ref, k_ref, v_ref, g_ref, sems):
    copies = [
        pltpu.make_async_copy(grads_ref.at[i], ref.at[0], sems.at[i])
        for i, ref in enumerate((q_ref, k_ref, v_ref))
    ]
    for copy in copies:
        copy.start()
    g_ref[...] = gain_ref[...]
    for copy in copies:
        copy.wait()


def local(query_rows, key_rows, value_rows, cotangent, norm_gain, doc_starts):
    anywhere = pl.BlockSpec(memory_space=pl.ANY)
    hbm = pl.BlockSpec(memory_space=pltpu.HBM)
    vmem = pl.BlockSpec(memory_space=pltpu.VMEM)
    smem = pl.BlockSpec(memory_space=pltpu.SMEM)
    dma = pltpu.SemaphoreType.DMA
    state = pltpu.VMEM((HEADS, DIM, DIM), F32)
    grads, gain_sum = pl.pallas_call(
        kernel,
        out_shape=(
            jax.ShapeDtypeStruct((3, ROWS, 8192), BF16),
            jax.ShapeDtypeStruct((8, DIM), F32),
        ),
        in_specs=[hbm] * 4 + [vmem, smem],
        out_specs=(anywhere, vmem),
        scratch_shapes=[
            pltpu.VMEM((4, TOK, COLS), BF16),
            pltpu.VMEM((TOK, TOK), F32),
            pltpu.VMEM((TOK, DIM), F32),
            pltpu.VMEM((TOK, DIM), F32),
            state, state, state, state, state,
            pltpu.VMEM((HEADS, TOK, TOK), F32),
            pltpu.VMEM((HEADS, TOK, DIM), BF16),
            pltpu.VMEM((HEADS, TOK, DIM), BF16),
            pltpu.VMEM((HEADS, TOK, DIM), F32),
            pltpu.VMEM((HEADS, TOK, DIM), F32),
            pltpu.VMEM((3, TOK, COLS), BF16),
            pltpu.VMEM((8, DIM), F32),
            pltpu.VMEM((4, 8, DIM), F32),
            pltpu.VMEM((SEQ, 8, DIM), F32),
            dma((4,)), dma((4,)), dma((NC,)), dma((NC,)), dma((NC,)), dma((NC,)), dma((3,)), dma((3,)),
            dma((4,)), dma((4,)), dma, dma,
        ],
        compiler_params=pltpu.CompilerParams(
            collective_id=1, has_side_effects=True, vmem_limit_bytes=60 * 1024 * 1024
        ),
        name="layer",
    )(key_rows, value_rows, query_rows, cotangent, norm_gain.reshape(8, DIM), doc_starts)
    rows = jax.ShapeDtypeStruct((1, ROWS, 8192), BF16)
    grad_q, grad_k, grad_v, gain = pl.pallas_call(
        place,
        out_shape=(rows, rows, rows, jax.ShapeDtypeStruct((8, DIM), F32)),
        in_specs=[vmem, vmem],
        out_specs=(anywhere, anywhere, anywhere, vmem),
        scratch_shapes=[dma((3,))],
        name="place",
    )(grads, gain_sum)
    return grad_q, grad_k, grad_v, gain.reshape(8 * DIM)


def solution(mesh):
    rows = P("dp", ("seq", "tensor"), None)
    return jax.shard_map(
        local,
        mesh=mesh,
        in_specs=(rows, rows, rows, rows, P("tensor"), P("dp", None)),
        out_specs=(rows, rows, rows, P("tensor")),
        check_vma=False,
    )
```

time: 727 us -> 123 us (0.17)
  the two profiles are of different devices: /device:TPU:4 before, /device:TPU:1 now
where the time goes in v1:
time: 123 us
  Pallas kernels  122 us (99%)
    pallas_call x1, Pallas kernels, local(): pl.pallas_call(kernel, out_shape=(jax.ShapeDtypeStruct((3, ROWS, 8192), B...  120 us
    pallas_call x1, Pallas kernels, local(): pl.pallas_call(place, out_shape=(rows, rows, rows, jax.ShapeDtypeStruct((...  2.63 us

profile of v1, /device:TPU:1, one launch (start us, length us, event | category | flops | bytes accessed | tf_op | source)
XLA Modules:
  0.0 123.0 jit_solution(8040787825270886494)
XLA Ops:
  0.6 119.8 %layer.1 = (bf16[3,16,8192]{2,1,0:T(8,128)(2,1)}, f32[8,128]{1,0:T(8,128)}) custom-call(bf16[1,16,8192]{2,1,0:T(8,128)(2,1)} %k_ref.1, bf16[1,16,8192]{2,1,0:T(8,128)(2,1)} %v_ref.1, bf16[1,16,8192]{2,1,0:T(8,128)(2,1)} %q_ref.1, bf16[1,16,8192]{2,1,0:T(8,128)(2,1)} %c_ref.1, f32[8,128]{1,0:T(8,128)} %bitcast.2, s32[1,8]{1,0:T(1,128)} %starts_ref.1), custom_call_target="tpu_custom_call" | custom-call | tf_op jit(solution)/shard_map/layer/pallas_call | solution.py:379
  120.4 2.6 %place.1 = (bf16[1,16,8192]{2,1,0:T(8,128)(2,1)}, bf16[1,16,8192]{2,1,0:T(8,128)(2,1)}, bf16[1,16,8192]{2,1,0:T(8,128)(2,1)}, f32[8,128]{1,0:T(8,128)}) custom-call(bf16[3,16,8192]{2,1,0:T(8,128)(2,1)} %get-tuple-element.10.grads_ref, f32[8,128]{1,0:T(8,128)} %get-tuple-element.11.gain_ref), custom_call_target="tpu_custom_call" | custom-call | tf_op jit(solution)/shard_map/place/pallas_call | solution.py:411

commit v2 on v1

v2 whole, which is shorter than its diff:
```python
import functools
import math

import jax
import jax.numpy as jnp
from jax import lax
from jax.experimental import pallas as pl
from jax.experimental.pallas import tpu as pltpu
from jax.sharding import PartitionSpec as P

MESH = pl.DeviceIdType.MESH
F32 = jnp.float32
BF16 = jnp.bfloat16
EPSILON = 1e-05
DIM = 128
HEADS = 2
GZ = 4
POS = 4
TOK = 512
HALF = 256
COLS = HEADS * DIM
ROWS = 16
GROUP = 32
SEQ = 16
SUB = 4
PIECE = DIM // SUB
NC = HEADS * SUB


def split(x):
    hi = x.astype(BF16)
    return hi, (x - hi.astype(F32)).astype(BF16)


def mm(a, b, ca=1, cb=0):
    return lax.dot_general(a, b, (((ca,), (cb,)), ((), ())), preferred_element_type=F32)


def kernel(
    k_ref, v_ref, q_ref, c_ref, gain_ref, starts_ref,
    out_ref, gout_ref,
    buf, mask, use, keep, own, fsend, rp, rm, sg, bsend, bm, bp, scores, dh, dl, dkl, dvl, obuf,
    gsrc, gy, gg, gz,
    in_send, in_recv, plus_send, rp_recv, minus_send, rm_recv, bminus_send, bm_recv, bplus_send, bp_recv,
    o_send, o_recv, gy_send, gy_recv, gg_send, gg_recv, gz_send, gz_recv,
):
    z, t, y = lax.axis_index("seq"), lax.axis_index("tensor"), lax.axis_index("dp")
    p, j = z // GZ, lax.rem(z, GZ)
    base = p * GZ
    me = j * 8 + t
    after, before = lax.rem(z + GZ, SEQ), lax.rem(z + SEQ - GZ, SEQ)

    def peer(s):
        g = lax.rem(me + s, GROUP)
        return g, g // 8, lax.rem(g, 8)

    barrier = pltpu.get_barrier_semaphore()

    def greet(zz, tt, yy):
        pl.semaphore_signal(barrier, inc=1, device_id=(zz, tt, yy), device_id_type=MESH)

    greet(after, t, y)
    greet(before, t, y)
    for s in range(1, 4):
        greet(z, t, lax.rem(y + s, 4))

    def greet_group(s, _):
        _, jj, tt = peer(s)
        greet(base + jj, tt, y)
        return 0

    lax.fori_loop(1, GROUP, greet_group, 0)

    def count(tok):
        total = jnp.zeros_like(tok)
        for i in range(8):
            total = total + (starts_ref[0, i] <= tok).astype(jnp.int32)
        return total

    first = base * 128
    prev = count(first - 1)
    last = count(first + TOK - 1)
    carry = (prev == last).astype(F32)
    far_in = (count(TOK - 1) == prev).astype(F32)
    far_out = (last == count(3 * TOK - 1)).astype(F32)
    row = lax.broadcasted_iota(jnp.int32, (TOK, DIM), 0) + first
    seg = count(row)
    use[...] = (seg == prev).astype(F32)
    keep[...] = (seg == last).astype(F32)
    seg_row = count(lax.broadcasted_iota(jnp.int32, (8, TOK), 1) + first)[:1]
    seg_col = jnp.concatenate([seg] * 4, axis=1)
    rows = lax.broadcasted_iota(jnp.int32, (TOK, TOK), 0)
    cols = lax.broadcasted_iota(jnp.int32, (TOK, TOK), 1)
    mask[...] = ((rows >= cols) & (seg_col == seg_row)).astype(F32)
    gsrc[...] = jnp.zeros_like(gsrc)

    @pl.when(p == 0)
    def _():
        rp[...] = jnp.zeros_like(rp)

    @pl.when(p <= 1)
    def _():
        rm[...] = jnp.zeros_like(rm)

    @pl.when(p == 3)
    def _():
        bm[...] = jnp.zeros_like(bm)

    @pl.when(p >= 2)
    def _():
        bp[...] = jnp.zeros_like(bp)

    pl.semaphore_wait(barrier, 31 + 2 + 3)

    mine = pl.ds(pl.multiple_of(me * ROWS, ROWS), ROWS)
    my_cols = pl.ds(pl.multiple_of(t * 1024 + j * COLS, COLS), COLS)

    def send_in(refs):
        def body(s, _):
            _, jj, tt = peer(s)
            col = pl.multiple_of(tt * 1024 + jj * COLS, COLS)
            for a, ref in refs:
                pltpu.make_async_remote_copy(
                    src_ref=ref.at[0, :, pl.ds(col, COLS)],
                    dst_ref=buf.at[a, mine, :],
                    send_sem=in_send.at[a],
                    recv_sem=in_recv.at[a],
                    device_id=(base + jj, tt, y),
                    device_id_type=MESH,
                ).start()
            return 0

        lax.fori_loop(1, GROUP, body, 0)
        for a, ref in refs:
            pltpu.make_async_copy(ref.at[0, :, my_cols], buf.at[a, mine, :], in_recv.at[a]).start()

    def wait_in(a):
        pltpu.make_async_copy(buf.at[a], buf.at[a], in_recv.at[a]).wait()

    send_in(((0, k_ref), (1, v_ref)))
    send_in(((2, q_ref), (3, c_ref)))

    def take(a, h, start=0, size=TOK):
        return buf[a, pl.ds(start, size), pl.ds(pl.multiple_of(h * DIM, DIM), DIM)]

    wait_in(0)
    wait_in(1)

    def local_state(h, _):
        kept = take(0, h) * keep[...].astype(BF16)
        own[h] = mm(kept, take(1, h), 0, 0)
        return 0

    lax.fori_loop(0, HEADS, local_state, 0)

    def piece(ref, c):
        return ref.at[c // SUB, pl.ds(pl.multiple_of(lax.rem(c, SUB) * PIECE, PIECE), PIECE), :]

    def move(src, dst, c, send, recv, to):
        return pltpu.make_async_remote_copy(
            src_ref=piece(src, c), dst_ref=piece(dst, c), send_sem=send.at[c], recv_sem=recv.at[c],
            device_id=(to, t, y), device_id_type=MESH,
        )

    def plus(src, c):
        return move(src, rp, c, plus_send, rp_recv, after)

    def minus(src, c):
        return move(src, rm, c, minus_send, rm_recv, before)

    def bminus(src, c):
        return move(src, bm, c, bminus_send, bm_recv, before)

    def bplus(src, c):
        return move(src, bp, c, bplus_send, bp_recv, after)

    def forward(c, _):
        @pl.when(p <= 1)
        def _():
            plus(own, c).start()

        @pl.when(p == 0)
        def _():
            minus(own, c).start()

        @pl.when(p == 2)
        def _():
            plus(own, c).wait_recv()
            piece(fsend, c)[...] = piece(own, c)[...] + carry * piece(rp, c)[...]
            plus(fsend, c).start()

        @pl.when(p == 3)
        def _():
            minus(rm, c).wait_recv()
            minus(rm, c).start()

        return 0

    def forward_rest(c, _):
        @pl.when((p == 1) | (p == 3))
        def _():
            plus(own, c).wait_recv()

        @pl.when(p == 2)
        def _():
            minus(rm, c).wait_recv()

        return 0

    def local_scores(h, _):
        for r in range(2):
            n = HALF * (r + 1)
            at = pl.ds(r * HALF, HALF)
            scores[h, at, pl.ds(0, n)] = (
                mm(take(2, h, r * HALF, HALF), take(0, h, 0, n), 1, 1) * mask[at, pl.ds(0, n)]
            )
        return 0

    def first_half(s, _):
        @pl.when((s == 0) == (p < 2))
        def _():
            lax.fori_loop(0, NC, forward, 0)

        @pl.when((s == 0) != (p < 2))
        def _():
            wait_in(2)
            lax.fori_loop(0, HEADS, local_scores, 0)

        return 0

    lax.fori_loop(0, 2, first_half, 0)
    wait_in(3)

    def attend(h, _):
        lax.fori_loop(h * SUB, h * SUB + SUB, forward_rest, 0)
        state = rp[h] + far_in * rm[h]
        rp[h] = state
        th, tl = split(state)
        at = j * HEADS + h
        gain = gain_ref[pl.ds(at, 1), :]
        gain_part = jnp.zeros((1, DIM), F32)
        state_grad = jnp.zeros((DIM, DIM), F32)
        for r in range(2):
            n = HALF * (r + 1)
            rr = pl.ds(r * HALF, HALF)
            query, value = take(2, h, r * HALF, HALF), take(1, h, 0, n)
            sh, sl = split(scores[h, rr, pl.ds(0, n)])
            used = use[rr, :]
            att = mm(sh, value) + mm(sl, value) + used * (mm(query, th) + mm(query, tl))
            centered = att - jnp.mean(att, axis=-1, keepdims=True)
            inv = lax.rsqrt(jnp.mean(centered * centered, axis=-1, keepdims=True) + EPSILON)
            normed = centered * inv
            up = take(3, h, r * HALF, HALF).astype(F32)
            gain_part = gain_part + jnp.sum(up * normed, axis=0, keepdims=True)
            dn = up * gain
            d_att = inv * (
                dn
                - jnp.mean(dn, axis=-1, keepdims=True)
                - normed * jnp.mean(dn * normed, axis=-1, keepdims=True)
            )
            hi, lo = split(d_att)
            dh[h, rr, :] = hi
            dl[h, rr, :] = lo
            used = used.astype(BF16)
            state_grad = state_grad + mm(query, hi * used, 0, 0) + mm(query, lo * used, 0, 0)
        gsrc[pl.ds(at, 1), :] = gain_part
        sg[h] = state_grad

        @pl.when(p >= 2)
        def _():
            for s in range(SUB):
                bminus(sg, h * SUB + s).start()

        @pl.when(p == 3)
        def _():
            for s in range(SUB):
                bplus(sg, h * SUB + s).start()

        return 0

    lax.fori_loop(0, HEADS, attend, 0)

    gy[y] = gsrc[...]

    def gy_copy(yy):
        return pltpu.make_async_remote_copy(
            src_ref=gy.at[y], dst_ref=gy.at[y], send_sem=gy_send.at[yy], recv_sem=gy_recv.at[y],
            device_id=(z, t, yy), device_id_type=MESH,
        )

    for s in range(1, 4):
        gy_copy(lax.rem(y + s, 4)).start()

    def backward(c, _):
        @pl.when(p == 1)
        def _():
            bminus(sg, c).wait_recv()
            piece(bsend, c)[...] = piece(sg, c)[...] + carry * piece(bm, c)[...]
            bminus(bsend, c).start()

        @pl.when(p == 0)
        def _():
            bplus(bp, c).wait_recv()
            bplus(bp, c).start()

        return 0

    def backward_rest(c, _):
        @pl.when((p == 0) | (p == 2))
        def _():
            bminus(sg, c).wait_recv()

        @pl.when(p == 1)
        def _():
            bplus(bp, c).wait_recv()

        return 0

    def send_out(i):
        def body(s, _):
            g, jj, tt = peer(s)
            pltpu.make_async_remote_copy(
                src_ref=obuf.at[i, pl.ds(pl.multiple_of(g * ROWS, ROWS), ROWS), :],
                dst_ref=out_ref.at[i, :, my_cols],
                send_sem=o_send.at[i],
                recv_sem=o_recv.at[i],
                device_id=(base + jj, tt, y),
                device_id_type=MESH,
            ).start()
            return 0

        lax.fori_loop(1, GROUP, body, 0)
        pltpu.make_async_copy(obuf.at[i, mine, :], out_ref.at[i, :, my_cols], o_recv.at[i]).start()

    def put(i, h, at, value):
        obuf[i, at, pl.ds(pl.multiple_of(h * DIM, DIM), DIM)] = value.astype(BF16)

    def local_grads(h, _):
        th, tl = split(rp[h])
        for r in range(2):
            n = HALF * (r + 1)
            rr, cc = pl.ds(r * HALF, HALF), pl.ds(0, n)
            key, value, query = take(0, h, 0, n), take(1, h, 0, n), take(2, h, r * HALF, HALF)
            hi, lo = dh[h, rr, :], dl[h, rr, :]
            d_sc = (mm(hi, value, 1, 1) + mm(lo, value, 1, 1)) * mask[rr, cc]
            eh, el = split(d_sc)
            sh, sl = split(scores[h, rr, cc])
            d_query = mm(eh, key) + mm(el, key)
            d_query = d_query + use[rr, :] * (mm(hi, th, 1, 1) + mm(hi, tl, 1, 1) + mm(lo, th, 1, 1))
            put(0, h, rr, d_query)
            d_key = mm(eh, query, 0, 0) + mm(el, query, 0, 0)
            d_value = mm(sh, hi, 0, 0) + mm(sl, hi, 0, 0) + mm(sh, lo, 0, 0)
            if r == 0:
                dkl[h, rr, :] = d_key
                dvl[h, rr, :] = d_value
            else:
                low = pl.ds(0, HALF)
                dkl[h, low, :] += d_key[:HALF]
                dvl[h, low, :] += d_value[:HALF]
                dkl[h, rr, :] = d_key[HALF:]
                dvl[h, rr, :] = d_value[HALF:]
        return 0

    def gg_copy(s):
        return pltpu.make_async_remote_copy(
            src_ref=gg.at[j], dst_ref=gg.at[j], send_sem=gg_send.at[s], recv_sem=gg_recv.at[j],
            device_id=(base + lax.rem(j + s, GZ), t, y), device_id_type=MESH,
        )

    def second_half(s, _):
        @pl.when((s == 0) == (p <= 1))
        def _():
            lax.fori_loop(0, HEADS, local_grads, 0)
            send_out(0)

        @pl.when((s == 0) != (p <= 1))
        def _():
            lax.fori_loop(0, NC, backward, 0)

        return 0

    lax.fori_loop(0, 2, second_half, 0)

    for s in range(1, 4):
        yy = lax.rem(y + s, 4)
        pltpu.make_async_copy(gy.at[yy], gy.at[yy], gy_recv.at[yy]).wait()
    gg[j] = (gy[0] + gy[1]) + (gy[2] + gy[3])
    for s in range(1, GZ):
        gg_copy(s).start()

    def last_grads(h, _):
        lax.fori_loop(h * SUB, h * SUB + SUB, backward_rest, 0)
        gh, gl = split(bm[h] + far_out * bp[h])
        key, value = take(0, h), take(1, h)
        everything = pl.ds(0, TOK)
        put(1, h, everything, dkl[h] + keep[...] * (mm(value, gh, 1, 1) + mm(value, gl, 1, 1)))
        put(2, h, everything, dvl[h] + keep[...] * (mm(key, gh) + mm(key, gl)))
        return 0

    lax.fori_loop(0, HEADS, last_grads, 0)
    send_out(1)
    send_out(2)

    for s in range(1, GZ):
        jj = lax.rem(j + s, GZ)
        pltpu.make_async_copy(gg.at[jj], gg.at[jj], gg_recv.at[jj]).wait()
    gz[0] = (gg[0] + gg[1]) + (gg[2] + gg[3])

    def gz_copy(i, partner):
        return pltpu.make_async_remote_copy(
            src_ref=gz.at[2 * i], dst_ref=gz.at[2 * i + 1], send_sem=gz_send.at[i], recv_sem=gz_recv.at[i],
            device_id=(partner, t, y), device_id_type=MESH,
        )

    even = lax.rem(p, 2) == 0
    near = jnp.where(even, after, before)
    other = jnp.where(even, before, after)
    gz_copy(0, near).start()
    gz_copy(0, near).wait_recv()
    gz[2] = gz[0] + gz[1]
    gz_copy(1, other).start()
    gz_copy(1, other).wait_recv()
    gout_ref[...] = (gz[2] + gz[3]) / math.sqrt(4 * SEQ * 128)

    for i in range(3):
        pltpu.make_async_copy(out_ref.at[i], out_ref.at[i], o_recv.at[i]).wait()
    for a in range(4):
        part = buf.at[a, pl.ds(0, TOK - ROWS), :]
        pltpu.make_async_copy(part, part, in_send.at[a]).wait()
    for i in range(3):
        part = obuf.at[i, pl.ds(0, TOK - ROWS), :]
        pltpu.make_async_copy(part, part, o_send.at[i]).wait()
    gz_copy(0, near).wait_send()
    gz_copy(1, other).wait_send()
    for s in range(1, GZ):
        gg_copy(s).wait_send()
    for s in range(1, 4):
        gy_copy(lax.rem(y + s, 4)).wait_send()

    def drain(c, _):
        @pl.when(p <= 2)
        def _():
            plus(own, c).wait_send()

        @pl.when((p == 0) | (p == 3))
        def _():
            minus(own, c).wait_send()
            bplus(sg, c).wait_send()

        @pl.when(p >= 1)
        def _():
            bminus(sg, c).wait_send()

        return 0

    lax.fori_loop(0, NC, drain, 0)


def place(grads_ref, gain_ref, q_ref, k_ref, v_ref, g_ref, sems):
    copies = [
        pltpu.make_async_copy(grads_ref.at[i], ref.at[0], sems.at[i])
        for i, ref in enumerate((q_ref, k_ref, v_ref))
    ]
    for copy in copies:
        copy.start()
    g_ref[...] = gain_ref[...]
    for copy in copies:
        copy.wait()


def local(query_rows, key_rows, value_rows, cotangent, norm_gain, doc_starts):
    anywhere = pl.BlockSpec(memory_space=pl.ANY)
    hbm = pl.BlockSpec(memory_space=pltpu.HBM)
    vmem = pl.BlockSpec(memory_space=pltpu.VMEM)
    smem = pl.BlockSpec(memory_space=pltpu.SMEM)
    dma = pltpu.SemaphoreType.DMA
    state = pltpu.VMEM((HEADS, DIM, DIM), F32)
    grads, gain_sum = pl.pallas_call(
        kernel,
        out_shape=(
            jax.ShapeDtypeStruct((3, ROWS, 8192), BF16),
            jax.ShapeDtypeStruct((8, DIM), F32),
        ),
        in_specs=[hbm] * 4 + [vmem, smem],
        out_specs=(anywhere, vmem),
        scratch_shapes=[
            pltpu.VMEM((4, TOK, COLS), BF16),
            pltpu.VMEM((TOK, TOK), F32),
            pltpu.VMEM((TOK, DIM), F32),
            pltpu.VMEM((TOK, DIM), F32),
            state, state, state, state, state, state, state, state,
            pltpu.VMEM((HEADS, TOK, TOK), F32),
            pltpu.VMEM((HEADS, TOK, DIM), BF16),
            pltpu.VMEM((HEADS, TOK, DIM), BF16),
            pltpu.VMEM((HEADS, TOK, DIM), F32),
            pltpu.VMEM((HEADS, TOK, DIM), F32),
            pltpu.VMEM((3, TOK, COLS), BF16),
            pltpu.VMEM((8, DIM), F32),
            pltpu.VMEM((4, 8, DIM), F32),
            pltpu.VMEM((GZ, 8, DIM), F32),
            pltpu.VMEM((4, 8, DIM), F32),
            dma((4,)), dma((4,)),
            dma((NC,)), dma((NC,)), dma((NC,)), dma((NC,)), dma((NC,)), dma((NC,)), dma((NC,)), dma((NC,)),
            dma((3,)), dma((3,)), dma((4,)), dma((4,)), dma((GZ,)), dma((GZ,)), dma((2,)), dma((2,)),
        ],
        compiler_params=pltpu.CompilerParams(
            collective_id=1, has_side_effects=True, vmem_limit_bytes=60 * 1024 * 1024
        ),
        name="layer",
    )(key_rows, value_rows, query_rows, cotangent, norm_gain.reshape(8, DIM), doc_starts)
    rows = jax.ShapeDtypeStruct((1, ROWS, 8192), BF16)
    grad_q, grad_k, grad_v, gain = pl.pallas_call(
        place,
        out_shape=(rows, rows, rows, jax.ShapeDtypeStruct((8, DIM), F32)),
        in_specs=[vmem, vmem],
        out_specs=(anywhere, anywhere, anywhere, vmem),
        scratch_shapes=[dma((3,))],
        name="place",
    )(grads, gain_sum)
    return grad_q, grad_k, grad_v, gain.reshape(8 * DIM)


def solution(mesh):
    rows = P("dp", ("seq", "tensor"), None)
    return jax.shard_map(
        local,
        mesh=mesh,
        in_specs=(rows, rows, rows, rows, P("tensor"), P("dp", None)),
        out_specs=(rows, rows, rows, P("tensor")),
        check_vma=False,
    )
```

time: 123 us -> 94.1 us (0.77)
  the two profiles are of different devices: /device:TPU:1 before, /device:TPU:64 now
where the time goes in v2:
time: 94.1 us; the launch traced here: 94 us
  Pallas kernels  93.3 us (99%)
    pallas_call x1, Pallas kernels, local(): pl.pallas_call(kernel, out_shape=(jax.ShapeDtypeStruct((3, ROWS, 8192), B...  90.7 us
    pallas_call x1, Pallas kernels, local(): pl.pallas_call(place, out_shape=(rows, rows, rows, jax.ShapeDtypeStruct((...  2.63 us

profile of v2, /device:TPU:64, one launch (start us, length us, event | category | flops | bytes accessed | tf_op | source)
XLA Modules:
  0.0 94.0 jit_solution(9543170255017759171)
XLA Ops:
  0.6 90.7 %layer.1 = (bf16[3,16,8192]{2,1,0:T(8,128)(2,1)}, f32[8,128]{1,0:T(8,128)}) custom-call(bf16[1,16,8192]{2,1,0:T(8,128)(2,1)} %k_ref.1, bf16[1,16,8192]{2,1,0:T(8,128)(2,1)} %v_ref.1, bf16[1,16,8192]{2,1,0:T(8,128)(2,1)} %q_ref.1, bf16[1,16,8192]{2,1,0:T(8,128)(2,1)} %c_ref.1, f32[8,128]{1,0:T(8,128)} %bitcast.2, s32[1,8]{1,0:T(1,128)} %starts_ref.1), custom_call_target="tpu_custom_call" | custom-call | tf_op jit(solution)/shard_map/layer/pallas_call | solution.py:478
  91.3 2.6 %place.1 = (bf16[1,16,8192]{2,1,0:T(8,128)(2,1)}, bf16[1,16,8192]{2,1,0:T(8,128)(2,1)}, bf16[1,16,8192]{2,1,0:T(8,128)(2,1)}, f32[8,128]{1,0:T(8,128)}) custom-call(bf16[3,16,8192]{2,1,0:T(8,128)(2,1)} %get-tuple-element.10.grads_ref, f32[8,128]{1,0:T(8,128)} %get-tuple-element.11.gain_ref), custom_call_target="tpu_custom_call" | custom-call | tf_op jit(solution)/shard_map/place/pallas_call | solution.py:512

commit v3 on v2

--- a/solution.py
+++ b/solution.py
@@ -22,9 +22,7 @@
 ROWS = 16
 GROUP = 32
 SEQ = 16
-SUB = 4
-PIECE = DIM // SUB
-NC = HEADS * SUB
+CODED = DIM + 16
 
 
 def split(x):
@@ -32,6 +30,19 @@
     return hi, (x - hi.astype(F32)).astype(BF16)
 
 
+def encode(x):
+    top = jnp.maximum(jnp.max(jnp.abs(x), axis=0, keepdims=True), 1e-30)
+    power = jnp.floor(jnp.log(top) * (1 / math.log(2)))
+    coded = jnp.clip(jnp.floor(x * jnp.exp2(14 - power) + 0.5), -32767, 32767)
+    rows = jnp.concatenate([coded, jnp.broadcast_to(power, (CODED - DIM, DIM))], axis=0)
+    return rows.astype(jnp.int32).astype(jnp.int16)
+
+
+def decode(coded):
+    values = coded.astype(jnp.int32).astype(F32)
+    return values[:DIM] * jnp.exp2(values[DIM : DIM + 1] - 14)
+
+
 def mm(a, b, ca=1, cb=0):
     return lax.dot_general(a, b, (((ca,), (cb,)), ((), ())), preferred_element_type=F32)
 
@@ -39,10 +50,11 @@
 def kernel(
     k_ref, v_ref, q_ref, c_ref, gain_ref, starts_ref,
     out_ref, gout_ref,
-    buf, mask, use, keep, own, fsend, rp, rm, sg, bsend, bm, bp, scores, dh, dl, dkl, dvl, obuf,
+    stage, kv, qc, mask, use, keep, own, own_c, fsend, rp, rm, states, sg, sg_c, bsend, bm, bp, scores, dh, dl, dkl, dvl, dq, dkv,
     gsrc, gy, gg, gz,
-    in_send, in_recv, plus_send, rp_recv, minus_send, rm_recv, bminus_send, bm_recv, bplus_send, bp_recv,
-    o_send, o_recv, gy_send, gy_recv, gg_send, gg_recv, gz_send, gz_recv,
+    st_sem, kv_send, kv_recv, qc_send, qc_recv,
+    plus_send, rp_recv, minus_send, rm_recv, bminus_send, bm_recv, bplus_send, bp_recv,
+    dq_send, dq_recv, dkv_send, dkv_recv, gy_send, gy_recv, gg_send, gg_recv, gz_send, gz_recv, ready, ready_y,
 ):
     z, t, y = lax.axis_index("seq"), lax.axis_index("tensor"), lax.axis_index("dp")
     p, j = z // GZ, lax.rem(z, GZ)
@@ -54,15 +66,30 @@
         g = lax.rem(me + s, GROUP)
         return g, g // 8, lax.rem(g, 8)
 
+    def staged(a, ref):
+        return pltpu.make_async_copy(ref.at[0], stage.at[a], st_sem.at[a])
+
+    rows_in = ((0, k_ref), (1, v_ref), (2, q_ref), (3, c_ref))
+    for a, ref in rows_in:
+        staged(a, ref).start()
+
     barrier = pltpu.get_barrier_semaphore()
 
     def greet(zz, tt, yy):
         pl.semaphore_signal(barrier, inc=1, device_id=(zz, tt, yy), device_id_type=MESH)
 
-    greet(after, t, y)
-    greet(before, t, y)
-    for s in range(1, 4):
-        greet(z, t, lax.rem(y + s, 4))
+    @pl.when(p < POS - 1)
+    def _():
+        greet(after, t, y)
+
+    @pl.when(p == 0)
+    def _():
+        greet(before, t, y)
+
+    for yy in range(1, 4):
+        @pl.when(yy > y)
+        def _():
+            greet(z, t, yy)
 
     def greet_group(s, _):
         _, jj, tt = peer(s)
@@ -110,55 +137,78 @@
     def _():
         bp[...] = jnp.zeros_like(bp)
 
-    pl.semaphore_wait(barrier, 31 + 2 + 3)
+    pl.semaphore_wait(barrier, 31 + y + (p + 1) // 2)
+
+    def answer(sem, zz, yy):
+        pl.semaphore_signal(sem, inc=1, device_id=(zz, t, yy), device_id_type=MESH)
+
+    @pl.when(p > 0)
+    def _():
+        answer(ready.at[0], before, y)
+
+    @pl.when(p == POS - 1)
+    def _():
+        answer(ready.at[1], after, y)
+
+    for yy in range(3):
+        @pl.when(yy < y)
+        def _():
+            answer(ready_y.at[y], z, yy)
 
     mine = pl.ds(pl.multiple_of(me * ROWS, ROWS), ROWS)
     my_cols = pl.ds(pl.multiple_of(t * 1024 + j * COLS, COLS), COLS)
 
-    def send_in(refs):
+    def to_heads(src, dst, jj, tt, send, recv):
+        return pltpu.make_async_remote_copy(
+            src_ref=src, dst_ref=dst, send_sem=send, recv_sem=recv,
+            device_id=(base + jj, tt, y), device_id_type=MESH,
+        )
+
+    def send_kv(s, _):
+        g, jj, tt = peer(s)
+        at = pl.ds(pl.multiple_of(tt * 1024 + jj * COLS, COLS), COLS)
+        to_heads(stage.at[pl.ds(0, 2), :, at], kv.at[:, mine, :], jj, tt, kv_send, kv_recv).start()
+        return 0
+
+    def send_qc(h):
         def body(s, _):
-            _, jj, tt = peer(s)
-            col = pl.multiple_of(tt * 1024 + jj * COLS, COLS)
-            for a, ref in refs:
-                pltpu.make_async_remote_copy(
-                    src_ref=ref.at[0, :, pl.ds(col, COLS)],
-                    dst_ref=buf.at[a, mine, :],
-                    send_sem=in_send.at[a],
-                    recv_sem=in_recv.at[a],
-                    device_id=(base + jj, tt, y),
-                    device_id_type=MESH,
-                ).start()
+            g, jj, tt = peer(s)
+            at = pl.ds(pl.multiple_of(tt * 1024 + jj * COLS + h * DIM, DIM), DIM)
+            to_heads(
+                stage.at[pl.ds(2, 2), :, at], qc.at[h, :, mine, :], jj, tt, qc_send.at[h], qc_recv.at[h]
+            ).start()
             return 0
 
         lax.fori_loop(1, GROUP, body, 0)
-        for a, ref in refs:
-            pltpu.make_async_copy(ref.at[0, :, my_cols], buf.at[a, mine, :], in_recv.at[a]).start()
-
-    def wait_in(a):
-        pltpu.make_async_copy(buf.at[a], buf.at[a], in_recv.at[a]).wait()
-
-    send_in(((0, k_ref), (1, v_ref)))
-    send_in(((2, q_ref), (3, c_ref)))
-
+        at = pl.ds(pl.multiple_of(t * 1024 + j * COLS + h * DIM, DIM), DIM)
+        pltpu.make_async_copy(stage.at[pl.ds(2, 2), :, at], qc.at[h, :, mine, :], qc_recv.at[h]).start()
+
+    staged(0, k_ref).wait()
+    staged(1, v_ref).wait()
+    lax.fori_loop(1, GROUP, send_kv, 0)
+    pltpu.make_async_copy(stage.at[pl.ds(0, 2), :, my_cols], kv.at[:, mine, :], kv_recv).start()
     def take(a, h, start=0, size=TOK):
-        return buf[a, pl.ds(start, size), pl.ds(pl.multiple_of(h * DIM, DIM), DIM)]
-
-    wait_in(0)
-    wait_in(1)
+        if a < 2:
+            return kv[a, pl.ds(start, size), pl.ds(pl.multiple_of(h * DIM, DIM), DIM)]
+        return qc[h, a - 2, pl.ds(start, size), :]
+
+    staged(2, q_ref).wait()
+    staged(3, c_ref).wait()
+    for h in range(HEADS):
+        send_qc(h)
+    pltpu.make_async_copy(kv, kv, kv_recv).wait()
 
     def local_state(h, _):
         kept = take(0, h) * keep[...].astype(BF16)
         own[h] = mm(kept, take(1, h), 0, 0)
+        own_c[h] = encode(own[h])
         return 0
 
     lax.fori_loop(0, HEADS, local_state, 0)
-
-    def piece(ref, c):
-        return ref.at[c // SUB, pl.ds(pl.multiple_of(lax.rem(c, SUB) * PIECE, PIECE), PIECE), :]
 
     def move(src, dst, c, send, recv, to):
         return pltpu.make_async_remote_copy(
-            src_ref=piece(src, c), dst_ref=piece(dst, c), send_sem=send.at[c], recv_sem=recv.at[c],
+            src_ref=src.at[c], dst_ref=dst.at[c], send_sem=send.at[c], recv_sem=recv.at[c],
             device_id=(to, t, y), device_id_type=MESH,
         )
 
@@ -177,16 +227,16 @@
     def forward(c, _):
         @pl.when(p <= 1)
         def _():
-            plus(own, c).start()
+            plus(own_c, c).start()
 
         @pl.when(p == 0)
         def _():
-            minus(own, c).start()
+            minus(own_c, c).start()
 
         @pl.when(p == 2)
         def _():
-            plus(own, c).wait_recv()
-            piece(fsend, c)[...] = piece(own, c)[...] + carry * piece(rp, c)[...]
+            plus(own_c, c).wait_recv()
+            fsend[c] = encode(own[c] + carry * decode(rp[c]))
             plus(fsend, c).start()
 
         @pl.when(p == 3)
@@ -199,7 +249,7 @@
     def forward_rest(c, _):
         @pl.when((p == 1) | (p == 3))
         def _():
-            plus(own, c).wait_recv()
+            plus(own_c, c).wait_recv()
 
         @pl.when(p == 2)
         def _():
@@ -216,25 +266,22 @@
             )
         return 0
 
-    def first_half(s, _):
-        @pl.when((s == 0) == (p < 2))
-        def _():
-            lax.fori_loop(0, NC, forward, 0)
-
-        @pl.when((s == 0) != (p < 2))
-        def _():
-            wait_in(2)
-            lax.fori_loop(0, HEADS, local_scores, 0)
-
-        return 0
-
-    lax.fori_loop(0, 2, first_half, 0)
-    wait_in(3)
+    @pl.when(p < POS - 1)
+    def _():
+        pl.semaphore_wait(ready.at[0], 1)
+
+    @pl.when(p == 0)
+    def _():
+        pl.semaphore_wait(ready.at[1], 1)
+
+    lax.fori_loop(0, HEADS, forward, 0)
 
     def attend(h, _):
-        lax.fori_loop(h * SUB, h * SUB + SUB, forward_rest, 0)
-        state = rp[h] + far_in * rm[h]
-        rp[h] = state
+        pltpu.make_async_copy(qc.at[h], qc.at[h], qc_recv.at[h]).wait()
+        local_scores(h, 0)
+        forward_rest(h, 0)
+        state = decode(rp[h]) + far_in * decode(rm[h])
+        states[h] = state
         th, tl = split(state)
         at = j * HEADS + h
         gain = gain_ref[pl.ds(at, 1), :]
@@ -265,16 +312,15 @@
             state_grad = state_grad + mm(query, hi * used, 0, 0) + mm(query, lo * used, 0, 0)
         gsrc[pl.ds(at, 1), :] = gain_part
         sg[h] = state_grad
+        sg_c[h] = encode(state_grad)
 
         @pl.when(p >= 2)
         def _():
-            for s in range(SUB):
-                bminus(sg, h * SUB + s).start()
+            bminus(sg_c, h).start()
 
         @pl.when(p == 3)
         def _():
-            for s in range(SUB):
-                bplus(sg, h * SUB + s).start()
+            bplus(sg_c, h).start()
 
         return 0
 
@@ -288,14 +334,19 @@
             device_id=(z, t, yy), device_id_type=MESH,
         )
 
+    for yy in range(1, 4):
+        @pl.when(yy > y)
+        def _():
+            pl.semaphore_wait(ready_y.at[yy], 1)
+
     for s in range(1, 4):
         gy_copy(lax.rem(y + s, 4)).start()
 
     def backward(c, _):
         @pl.when(p == 1)
         def _():
-            bminus(sg, c).wait_recv()
-            piece(bsend, c)[...] = piece(sg, c)[...] + carry * piece(bm, c)[...]
+            bminus(sg_c, c).wait_recv()
+            bsend[c] = encode(sg[c] + carry * decode(bm[c]))
             bminus(bsend, c).start()
 
         @pl.when(p == 0)
@@ -308,7 +359,7 @@
     def backward_rest(c, _):
         @pl.when((p == 0) | (p == 2))
         def _():
-            bminus(sg, c).wait_recv()
+            bminus(sg_c, c).wait_recv()
 
         @pl.when(p == 1)
         def _():
@@ -316,27 +367,28 @@
 
         return 0
 
-    def send_out(i):
+    def send_dq(s, _):
+        g, jj, tt = peer(s)
+        at = pl.ds(pl.multiple_of(g * ROWS, ROWS), ROWS)
+        to_heads(dq.at[at, :], out_ref.at[0, :, my_cols], jj, tt, dq_send, dq_recv).start()
+        return 0
+
+    def send_dkv(h):
+        cols = pl.ds(pl.multiple_of(t * 1024 + j * COLS + h * DIM, DIM), DIM)
+
         def body(s, _):
             g, jj, tt = peer(s)
-            pltpu.make_async_remote_copy(
-                src_ref=obuf.at[i, pl.ds(pl.multiple_of(g * ROWS, ROWS), ROWS), :],
-                dst_ref=out_ref.at[i, :, my_cols],
-                send_sem=o_send.at[i],
-                recv_sem=o_recv.at[i],
-                device_id=(base + jj, tt, y),
-                device_id_type=MESH,
+            at = pl.ds(pl.multiple_of(g * ROWS, ROWS), ROWS)
+            to_heads(
+                dkv.at[h, :, at, :], out_ref.at[pl.ds(1, 2), :, cols], jj, tt, dkv_send.at[h], dkv_recv.at[h]
             ).start()
             return 0
 
         lax.fori_loop(1, GROUP, body, 0)
-        pltpu.make_async_copy(obuf.at[i, mine, :], out_ref.at[i, :, my_cols], o_recv.at[i]).start()
-
-    def put(i, h, at, value):
-        obuf[i, at, pl.ds(pl.multiple_of(h * DIM, DIM), DIM)] = value.astype(BF16)
+        pltpu.make_async_copy(dkv.at[h, :, mine, :], out_ref.at[pl.ds(1, 2), :, cols], dkv_recv.at[h]).start()
 
     def local_grads(h, _):
-        th, tl = split(rp[h])
+        th, tl = split(states[h])
         for r in range(2):
             n = HALF * (r + 1)
             rr, cc = pl.ds(r * HALF, HALF), pl.ds(0, n)
@@ -347,7 +399,7 @@
             sh, sl = split(scores[h, rr, cc])
             d_query = mm(eh, key) + mm(el, key)
             d_query = d_query + use[rr, :] * (mm(hi, th, 1, 1) + mm(hi, tl, 1, 1) + mm(lo, th, 1, 1))
-            put(0, h, rr, d_query)
+            dq[rr, pl.ds(pl.multiple_of(h * DIM, DIM), DIM)] = d_query.astype(BF16)
             d_key = mm(eh, query, 0, 0) + mm(el, query, 0, 0)
             d_value = mm(sh, hi, 0, 0) + mm(sl, hi, 0, 0) + mm(sh, lo, 0, 0)
             if r == 0:
@@ -367,19 +419,9 @@
             device_id=(base + lax.rem(j + s, GZ), t, y), device_id_type=MESH,
         )
 
-    def second_half(s, _):
-        @pl.when((s == 0) == (p <= 1))
-        def _():
-            lax.fori_loop(0, HEADS, local_grads, 0)
-            send_out(0)
-
-        @pl.when((s == 0) != (p <= 1))
-        def _():
-            lax.fori_loop(0, NC, backward, 0)
-
-        return 0
-
-    lax.fori_loop(0, 2, second_half, 0)
+    lax.fori_loop(0, HEADS, local_grads, 0)
+    lax.fori_loop(1, GROUP, send_dq, 0)
+    pltpu.make_async_copy(dq.at[mine, :], out_ref.at[0, :, my_cols], dq_recv).start()
 
     for s in range(1, 4):
         yy = lax.rem(y + s, 4)
@@ -388,23 +430,11 @@
     for s in range(1, GZ):
         gg_copy(s).start()
 
-    def last_grads(h, _):
-        lax.fori_loop(h * SUB, h * SUB + SUB, backward_rest, 0)
-        gh, gl = split(bm[h] + far_out * bp[h])
-        key, value = take(0, h), take(1, h)
-        everything = pl.ds(0, TOK)
-        put(1, h, everything, dkl[h] + keep[...] * (mm(value, gh, 1, 1) + mm(value, gl, 1, 1)))
-        put(2, h, everything, dvl[h] + keep[...] * (mm(key, gh) + mm(key, gl)))
-        return 0
-
-    lax.fori_loop(0, HEADS, last_grads, 0)
-    send_out(1)
-    send_out(2)
-
-    for s in range(1, GZ):
-        jj = lax.rem(j + s, GZ)
-        pltpu.make_async_copy(gg.at[jj], gg.at[jj], gg_recv.at[jj]).wait()
-    gz[0] = (gg[0] + gg[1]) + (gg[2] + gg[3])
+    lax.fori_loop(0, HEADS, backward, 0)
+
+    even = lax.rem(p, 2) == 0
+    near = jnp.where(even, after, before)
+    other = jnp.where(even, before, after)
 
     def gz_copy(i, partner):
         return pltpu.make_async_remote_copy(
@@ -412,24 +442,42 @@
             device_id=(partner, t, y), device_id_type=MESH,
         )
 
-    even = lax.rem(p, 2) == 0
-    near = jnp.where(even, after, before)
-    other = jnp.where(even, before, after)
-    gz_copy(0, near).start()
+    def last_grads(h, _):
+        backward_rest(h, 0)
+        gh, gl = split(decode(bm[h]) + far_out * decode(bp[h]))
+        key, value = take(0, h), take(1, h)
+        d_key = dkl[h] + keep[...] * (mm(value, gh, 1, 1) + mm(value, gl, 1, 1))
+        d_value = dvl[h] + keep[...] * (mm(key, gh) + mm(key, gl))
+        dkv[h, 0] = d_key.astype(BF16)
+        dkv[h, 1] = d_value.astype(BF16)
+        send_dkv(h)
+
+        @pl.when(h == 0)
+        def _():
+            for s in range(1, GZ):
+                jj = lax.rem(j + s, GZ)
+                pltpu.make_async_copy(gg.at[jj], gg.at[jj], gg_recv.at[jj]).wait()
+            gz[0] = (gg[0] + gg[1]) + (gg[2] + gg[3])
+            gz_copy(0, near).start()
+
+        return 0
+
+    lax.fori_loop(0, HEADS, last_grads, 0)
     gz_copy(0, near).wait_recv()
     gz[2] = gz[0] + gz[1]
     gz_copy(1, other).start()
     gz_copy(1, other).wait_recv()
     gout_ref[...] = (gz[2] + gz[3]) / math.sqrt(4 * SEQ * 128)
 
-    for i in range(3):
-        pltpu.make_async_copy(out_ref.at[i], out_ref.at[i], o_recv.at[i]).wait()
-    for a in range(4):
-        part = buf.at[a, pl.ds(0, TOK - ROWS), :]
-        pltpu.make_async_copy(part, part, in_send.at[a]).wait()
-    for i in range(3):
-        part = obuf.at[i, pl.ds(0, TOK - ROWS), :]
-        pltpu.make_async_copy(part, part, o_send.at[i]).wait()
+    pltpu.make_async_copy(out_ref.at[0], out_ref.at[0], dq_recv).wait()
+    for h in range(HEADS):
+        pltpu.make_async_copy(out_ref.at[1 + h], out_ref.at[1 + h], dkv_recv.at[h]).wait()
+    most = pl.ds(0, TOK - ROWS)
+    pltpu.make_async_copy(kv.at[:, most, :], kv.at[:, most, :], kv_send).wait()
+    pltpu.make_async_copy(dq.at[most, :], dq.at[most, :], dq_send).wait()
+    for h in range(HEADS):
+        pltpu.make_async_copy(qc.at[h, :, most, :], qc.at[h, :, most, :], qc_send.at[h]).wait()
+        pltpu.make_async_copy(dkv.at[h, :, most, :], dkv.at[h, :, most, :], dkv_send.at[h]).wait()
     gz_copy(0, near).wait_send()
     gz_copy(1, other).wait_send()
     for s in range(1, GZ):
@@ -440,20 +488,20 @@
     def drain(c, _):
         @pl.when(p <= 2)
         def _():
-            plus(own, c).wait_send()
+            plus(own_c, c).wait_send()
 
         @pl.when((p == 0) | (p == 3))
         def _():
-            minus(own, c).wait_send()
-            bplus(sg, c).wait_send()
+            minus(own_c, c).wait_send()
+            bplus(sg_c, c).wait_send()
 
         @pl.when(p >= 1)
         def _():
-            bminus(sg, c).wait_send()
-
-        return 0
-
-    lax.fori_loop(0, NC, drain, 0)
+            bminus(sg_c, c).wait_send()
+
+        return 0
+
+    lax.fori_loop(0, HEADS, drain, 0)
 
 
 def place(grads_ref, gain_ref, q_ref, k_ref, v_ref, g_ref, sems):
@@ -475,6 +523,7 @@
     smem = pl.BlockSpec(memory_space=pltpu.SMEM)
     dma = pltpu.SemaphoreType.DMA
     state = pltpu.VMEM((HEADS, DIM, DIM), F32)
+    coded = pltpu.VMEM((HEADS, CODED, DIM), jnp.int16)
     grads, gain_sum = pl.pallas_call(
         kernel,
         out_shape=(
@@ -484,24 +533,30 @@
         in_specs=[hbm] * 4 + [vmem, smem],
         out_specs=(anywhere, vmem),
         scratch_shapes=[
-            pltpu.VMEM((4, TOK, COLS), BF16),
+            pltpu.VMEM((4, ROWS, 8192), BF16),
+            pltpu.VMEM((2, TOK, COLS), BF16),
+            pltpu.VMEM((HEADS, 2, TOK, DIM), BF16),
             pltpu.VMEM((TOK, TOK), F32),
             pltpu.VMEM((TOK, DIM), F32),
             pltpu.VMEM((TOK, DIM), F32),
-            state, state, state, state, state, state, state, state,
+            state, coded, coded, coded, coded, state, state, coded, coded, coded, coded,
             pltpu.VMEM((HEADS, TOK, TOK), F32),
             pltpu.VMEM((HEADS, TOK, DIM), BF16),
             pltpu.VMEM((HEADS, TOK, DIM), BF16),
             pltpu.VMEM((HEADS, TOK, DIM), F32),
             pltpu.VMEM((HEADS, TOK, DIM), F32),
-            pltpu.VMEM((3, TOK, COLS), BF16),
+            pltpu.VMEM((TOK, COLS), BF16),
+            pltpu.VMEM((HEADS, 2, TOK, DIM), BF16),
             pltpu.VMEM((8, DIM), F32),
             pltpu.VMEM((4, 8, DIM), F32),
             pltpu.VMEM((GZ, 8, DIM), F32),
             pltpu.VMEM((4, 8, DIM), F32),
-            dma((4,)), dma((4,)),
-            dma((NC,)), dma((NC,)), dma((NC,)), dma((NC,)), dma((NC,)), dma((NC,)), dma((NC,)), dma((NC,)),
-            dma((3,)), dma((3,)), dma((4,)), dma((4,)), dma((GZ,)), dma((GZ,)), dma((2,)), dma((2,)),
+            dma((4,)), dma, dma, dma((HEADS,)), dma((HEADS,)),
+            dma((HEADS,)), dma((HEADS,)), dma((HEADS,)), dma((HEADS,)),
+            dma((HEADS,)), dma((HEADS,)), dma((HEADS,)), dma((HEADS,)),
+            dma, dma, dma((HEADS,)), dma((HEADS,)),
+            dma((4,)), dma((4,)), dma((GZ,)), dma((GZ,)), dma((2,)), dma((2,)),
+            pltpu.SemaphoreType.REGULAR((2,)), pltpu.SemaphoreType.REGULAR((4,)),
         ],
         compiler_params=pltpu.CompilerParams(
             collective_id=1, has_side_effects=True, vmem_limit_bytes=60 * 1024 * 1024

time: 94.1 us -> 80.5 us (0.86)
  the two profiles are of different devices: /device:TPU:64 before, /device:TPU:1 now
where the time goes in v3:
time: 80.5 us; the launch traced here: 80.1 us
  Pallas kernels  79.4 us (99%)
    pallas_call x1, Pallas kernels, local(): pl.pallas_call(kernel, out_shape=(jax.ShapeDtypeStruct((3, ROWS, 8192), B...  76.8 us
    pallas_call x1, Pallas kernels, local(): pl.pallas_call(place, out_shape=(rows, rows, rows, jax.ShapeDtypeStruct((...  2.63 us

profile of v3, /device:TPU:1, one launch (start us, length us, event | category | flops | bytes accessed | tf_op | source)
XLA Modules:
  0.0 80.1 jit_solution(2276960343124812988)
XLA Ops:
  0.6 76.8 %layer.1 = (bf16[3,16,8192]{2,1,0:T(8,128)(2,1)}, f32[8,128]{1,0:T(8,128)}) custom-call(bf16[1,16,8192]{2,1,0:T(8,128)(2,1)} %k_ref.1, bf16[1,16,8192]{2,1,0:T(8,128)(2,1)} %v_ref.1, bf16[1,16,8192]{2,1,0:T(8,128)(2,1)} %q_ref.1, bf16[1,16,8192]{2,1,0:T(8,128)(2,1)} %c_ref.1, f32[8,128]{1,0:T(8,128)} %bitcast.2, s32[1,8]{1,0:T(1,128)} %starts_ref.1), custom_call_target="tpu_custom_call" | custom-call | tf_op jit(solution)/shard_map/layer/pallas_call | solution.py:527
  77.4 2.6 %place.1 = (bf16[1,16,8192]{2,1,0:T(8,128)(2,1)}, bf16[1,16,8192]{2,1,0:T(8,128)(2,1)}, bf16[1,16,8192]{2,1,0:T(8,128)(2,1)}, f32[8,128]{1,0:T(8,128)}) custom-call(bf16[3,16,8192]{2,1,0:T(8,128)(2,1)} %get-tuple-element.10.grads_ref, f32[8,128]{1,0:T(8,128)} %get-tuple-element.11.gain_ref), custom_call_target="tpu_custom_call" | custom-call | tf_op jit(solution)/shard_map/place/pallas_call | solution.py:567

commit v4 on v3

--- a/solution.py
+++ b/solution.py
@@ -48,13 +48,13 @@
 
 
 def kernel(
-    k_ref, v_ref, q_ref, c_ref, gain_ref, starts_ref,
+    k_ref, v_ref, q_ref, c_ref, gain_in, starts_in,
     out_ref, gout_ref,
-    stage, kv, qc, mask, use, keep, own, own_c, fsend, rp, rm, states, sg, sg_c, bsend, bm, bp, scores, dh, dl, dkl, dvl, dq, dkv,
+    stage, kv, qc, mask, use, keep, own, own_c, fsend, rp, rm, states, sg_c, b1, b2, b3, inner, scores, dh, dl, dkl, dvl, dq, dkv,
     gsrc, gy, gg, gz,
     st_sem, kv_send, kv_recv, qc_send, qc_recv,
-    plus_send, rp_recv, minus_send, rm_recv, bminus_send, bm_recv, bplus_send, bp_recv,
-    dq_send, dq_recv, dkv_send, dkv_recv, gy_send, gy_recv, gg_send, gg_recv, gz_send, gz_recv, ready, ready_y,
+    plus_send, rp_recv, minus_send, rm_recv, b1_send, b1_recv, b2_send, b2_recv, b3_send, b3_recv,
+    dq_send, dq_recv, dkv_send, dkv_recv, gy_send, gy_recv, gg_send, gg_recv, gz_send, gz_recv, ready, ready_y, gain_ref, starts_ref, small_sem,
 ):
     z, t, y = lax.axis_index("seq"), lax.axis_index("tensor"), lax.axis_index("dp")
     p, j = z // GZ, lax.rem(z, GZ)
@@ -73,18 +73,22 @@
     for a, ref in rows_in:
         staged(a, ref).start()
 
+    small = (
+        pltpu.make_async_copy(gain_in, gain_ref, small_sem.at[0]),
+        pltpu.make_async_copy(starts_in, starts_ref, small_sem.at[1]),
+    )
+    for copy in small:
+        copy.start()
+
     barrier = pltpu.get_barrier_semaphore()
 
     def greet(zz, tt, yy):
         pl.semaphore_signal(barrier, inc=1, device_id=(zz, tt, yy), device_id_type=MESH)
 
-    @pl.when(p < POS - 1)
-    def _():
-        greet(after, t, y)
-
-    @pl.when(p == 0)
-    def _():
-        greet(before, t, y)
+    for d in range(1, POS):
+        @pl.when(p + d < POS)
+        def _():
+            greet(lax.rem(z + d * GZ, SEQ), t, y)
 
     for yy in range(1, 4):
         @pl.when(yy > y)
@@ -97,6 +101,67 @@
         return 0
 
     lax.fori_loop(1, GROUP, greet_group, 0)
+
+    pl.semaphore_wait(barrier, 31 + y + p)
+
+    def answer(sem, zz, yy):
+        pl.semaphore_signal(sem, inc=1, device_id=(zz, t, yy), device_id_type=MESH)
+
+    @pl.when(p > 0)
+    def _():
+        answer(ready.at[0], before, y)
+
+    @pl.when(p == POS - 1)
+    def _():
+        answer(ready.at[1], after, y)
+
+    for yy in range(3):
+        @pl.when(yy < y)
+        def _():
+            answer(ready_y.at[y], z, yy)
+
+    mine = pl.ds(pl.multiple_of(me * ROWS, ROWS), ROWS)
+    my_cols = pl.ds(pl.multiple_of(t * 1024 + j * COLS, COLS), COLS)
+
+    def to_heads(src, dst, jj, tt, send, recv):
+        return pltpu.make_async_remote_copy(
+            src_ref=src, dst_ref=dst, send_sem=send, recv_sem=recv,
+            device_id=(base + jj, tt, y), device_id_type=MESH,
+        )
+
+    def send_in(first_row, dst, send, recv, h):
+        def part(tt, jj):
+            cols = pl.ds(pl.multiple_of(tt * 1024 + jj * COLS + h * DIM, DIM), DIM)
+            return stage.at[pl.ds(first_row, 2), :, cols]
+
+        def body(s, _):
+            g, jj, tt = peer(s)
+            to_heads(part(tt, jj), dst.at[h, :, mine, :], jj, tt, send.at[h], recv.at[h]).start()
+            return 0
+
+        lax.fori_loop(1, GROUP, body, 0)
+        pltpu.make_async_copy(part(t, j), dst.at[h, :, mine, :], recv.at[h]).start()
+
+    def send_kv(h):
+        send_in(0, kv, kv_send, kv_recv, h)
+
+    def send_qc(h):
+        send_in(2, qc, qc_send, qc_recv, h)
+
+    staged(0, k_ref).wait()
+    staged(1, v_ref).wait()
+    send_kv(0)
+    staged(2, q_ref).wait()
+    staged(3, c_ref).wait()
+
+    @pl.when(p >= 2)
+    def _():
+        send_qc(0)
+
+    def take(a, h, start=0, size=TOK):
+        if a < 2:
+            return kv[h, a, pl.ds(start, size), :]
+        return qc[h, a - 2, pl.ds(start, size), :]
 
     def count(tok):
         total = jnp.zeros_like(tok)
@@ -104,12 +169,15 @@
             total = total + (starts_ref[0, i] <= tok).astype(jnp.int32)
         return total
 
+    for copy in small:
+        copy.wait()
     first = base * 128
     prev = count(first - 1)
     last = count(first + TOK - 1)
     carry = (prev == last).astype(F32)
     far_in = (count(TOK - 1) == prev).astype(F32)
-    far_out = (last == count(3 * TOK - 1)).astype(F32)
+    out2 = (last == count(first + 2 * TOK - 1)).astype(F32)
+    out3 = (last == count(first + 3 * TOK - 1)).astype(F32)
     row = lax.broadcasted_iota(jnp.int32, (TOK, DIM), 0) + first
     seg = count(row)
     use[...] = (seg == prev).astype(F32)
@@ -131,72 +199,16 @@
 
     @pl.when(p == 3)
     def _():
-        bm[...] = jnp.zeros_like(bm)
+        b1[...] = jnp.zeros_like(b1)
 
     @pl.when(p >= 2)
     def _():
-        bp[...] = jnp.zeros_like(bp)
-
-    pl.semaphore_wait(barrier, 31 + y + (p + 1) // 2)
-
-    def answer(sem, zz, yy):
-        pl.semaphore_signal(sem, inc=1, device_id=(zz, t, yy), device_id_type=MESH)
-
-    @pl.when(p > 0)
-    def _():
-        answer(ready.at[0], before, y)
-
-    @pl.when(p == POS - 1)
-    def _():
-        answer(ready.at[1], after, y)
-
-    for yy in range(3):
-        @pl.when(yy < y)
-        def _():
-            answer(ready_y.at[y], z, yy)
-
-    mine = pl.ds(pl.multiple_of(me * ROWS, ROWS), ROWS)
-    my_cols = pl.ds(pl.multiple_of(t * 1024 + j * COLS, COLS), COLS)
-
-    def to_heads(src, dst, jj, tt, send, recv):
-        return pltpu.make_async_remote_copy(
-            src_ref=src, dst_ref=dst, send_sem=send, recv_sem=recv,
-            device_id=(base + jj, tt, y), device_id_type=MESH,
-        )
-
-    def send_kv(s, _):
-        g, jj, tt = peer(s)
-        at = pl.ds(pl.multiple_of(tt * 1024 + jj * COLS, COLS), COLS)
-        to_heads(stage.at[pl.ds(0, 2), :, at], kv.at[:, mine, :], jj, tt, kv_send, kv_recv).start()
-        return 0
-
-    def send_qc(h):
-        def body(s, _):
-            g, jj, tt = peer(s)
-            at = pl.ds(pl.multiple_of(tt * 1024 + jj * COLS + h * DIM, DIM), DIM)
-            to_heads(
-                stage.at[pl.ds(2, 2), :, at], qc.at[h, :, mine, :], jj, tt, qc_send.at[h], qc_recv.at[h]
-            ).start()
-            return 0
-
-        lax.fori_loop(1, GROUP, body, 0)
-        at = pl.ds(pl.multiple_of(t * 1024 + j * COLS + h * DIM, DIM), DIM)
-        pltpu.make_async_copy(stage.at[pl.ds(2, 2), :, at], qc.at[h, :, mine, :], qc_recv.at[h]).start()
-
-    staged(0, k_ref).wait()
-    staged(1, v_ref).wait()
-    lax.fori_loop(1, GROUP, send_kv, 0)
-    pltpu.make_async_copy(stage.at[pl.ds(0, 2), :, my_cols], kv.at[:, mine, :], kv_recv).start()
-    def take(a, h, start=0, size=TOK):
-        if a < 2:
-            return kv[a, pl.ds(start, size), pl.ds(pl.multiple_of(h * DIM, DIM), DIM)]
-        return qc[h, a - 2, pl.ds(start, size), :]
-
-    staged(2, q_ref).wait()
-    staged(3, c_ref).wait()
-    for h in range(HEADS):
-        send_qc(h)
-    pltpu.make_async_copy(kv, kv, kv_recv).wait()
+        b2[...] = jnp.zeros_like(b2)
+
+    @pl.when(p >= 1)
+    def _():
+        b3[...] = jnp.zeros_like(b3)
+
 
     def local_state(h, _):
         kept = take(0, h) * keep[...].astype(BF16)
@@ -204,7 +216,6 @@
         own_c[h] = encode(own[h])
         return 0
 
-    lax.fori_loop(0, HEADS, local_state, 0)
 
     def move(src, dst, c, send, recv, to):
         return pltpu.make_async_remote_copy(
@@ -218,11 +229,14 @@
     def minus(src, c):
         return move(src, rm, c, minus_send, rm_recv, before)
 
-    def bminus(src, c):
-        return move(src, bm, c, bminus_send, bm_recv, before)
-
-    def bplus(src, c):
-        return move(src, bp, c, bplus_send, bp_recv, after)
+    def back1(c):
+        return move(sg_c, b1, c, b1_send, b1_recv, before)
+
+    def back2(c):
+        return move(sg_c, b2, c, b2_send, b2_recv, lax.rem(z + SEQ - 2 * GZ, SEQ))
+
+    def back3(c):
+        return move(sg_c, b3, c, b3_send, b3_recv, after)
 
     def forward(c, _):
         @pl.when(p <= 1)
@@ -264,17 +278,10 @@
             scores[h, at, pl.ds(0, n)] = (
                 mm(take(2, h, r * HALF, HALF), take(0, h, 0, n), 1, 1) * mask[at, pl.ds(0, n)]
             )
-        return 0
-
-    @pl.when(p < POS - 1)
-    def _():
-        pl.semaphore_wait(ready.at[0], 1)
-
-    @pl.when(p == 0)
-    def _():
-        pl.semaphore_wait(ready.at[1], 1)
-
-    lax.fori_loop(0, HEADS, forward, 0)
+            sh, sl = split(scores[h, at, pl.ds(0, n)])
+            value = take(1, h, 0, n)
+            inner[h, at, :] = mm(sh, value) + mm(sl, value)
+        return 0
 
     def attend(h, _):
         pltpu.make_async_copy(qc.at[h], qc.at[h], qc_recv.at[h]).wait()
@@ -290,10 +297,9 @@
         for r in range(2):
             n = HALF * (r + 1)
             rr = pl.ds(r * HALF, HALF)
-            query, value = take(2, h, r * HALF, HALF), take(1, h, 0, n)
-            sh, sl = split(scores[h, rr, pl.ds(0, n)])
+            query = take(2, h, r * HALF, HALF)
             used = use[rr, :]
-            att = mm(sh, value) + mm(sl, value) + used * (mm(query, th) + mm(query, tl))
+            att = inner[h, rr, :] + used * (mm(query, th) + mm(query, tl))
             centered = att - jnp.mean(att, axis=-1, keepdims=True)
             inv = lax.rsqrt(jnp.mean(centered * centered, axis=-1, keepdims=True) + EPSILON)
             normed = centered * inv
@@ -311,20 +317,52 @@
             used = used.astype(BF16)
             state_grad = state_grad + mm(query, hi * used, 0, 0) + mm(query, lo * used, 0, 0)
         gsrc[pl.ds(at, 1), :] = gain_part
-        sg[h] = state_grad
         sg_c[h] = encode(state_grad)
 
+        @pl.when(p == 3)
+        def _():
+            back3(h).start()
+
         @pl.when(p >= 2)
         def _():
-            bminus(sg_c, h).start()
-
-        @pl.when(p == 3)
-        def _():
-            bplus(sg_c, h).start()
-
-        return 0
-
-    lax.fori_loop(0, HEADS, attend, 0)
+            back2(h).start()
+
+        @pl.when(p >= 1)
+        def _():
+            back1(h).start()
+
+        return 0
+
+    def states_of(h, _):
+        pltpu.make_async_copy(kv.at[h], kv.at[h], kv_recv.at[h]).wait()
+        local_state(h, 0)
+
+        @pl.when((h == 0) & (p < POS - 1))
+        def _():
+            pl.semaphore_wait(ready.at[0], 1)
+
+        @pl.when((h == 0) & (p == 0))
+        def _():
+            pl.semaphore_wait(ready.at[1], 1)
+
+        forward(h, 0)
+
+        @pl.when(p <= 1)
+        def _():
+            send_qc(h)
+
+        @pl.when(h == 0)
+        def _():
+            send_kv(1)
+
+        @pl.when((h == 0) & (p >= 2))
+        def _():
+            send_qc(1)
+
+        attend(h, 0)
+        return 0
+
+    lax.fori_loop(0, HEADS, states_of, 0)
 
     gy[y] = gsrc[...]
 
@@ -343,35 +381,31 @@
         gy_copy(lax.rem(y + s, 4)).start()
 
     def backward(c, _):
-        @pl.when(p == 1)
-        def _():
-            bminus(sg_c, c).wait_recv()
-            bsend[c] = encode(sg[c] + carry * decode(bm[c]))
-            bminus(bsend, c).start()
+        @pl.when(p <= 2)
+        def _():
+            back1(c).wait_recv()
+
+        @pl.when(p <= 1)
+        def _():
+            back2(c).wait_recv()
 
         @pl.when(p == 0)
         def _():
-            bplus(bp, c).wait_recv()
-            bplus(bp, c).start()
-
-        return 0
-
-    def backward_rest(c, _):
-        @pl.when((p == 0) | (p == 2))
-        def _():
-            bminus(sg_c, c).wait_recv()
-
-        @pl.when(p == 1)
-        def _():
-            bplus(bp, c).wait_recv()
-
-        return 0
-
-    def send_dq(s, _):
-        g, jj, tt = peer(s)
-        at = pl.ds(pl.multiple_of(g * ROWS, ROWS), ROWS)
-        to_heads(dq.at[at, :], out_ref.at[0, :, my_cols], jj, tt, dq_send, dq_recv).start()
-        return 0
+            back3(c).wait_recv()
+
+        return 0
+
+    def send_dq(h):
+        cols = pl.ds(pl.multiple_of(t * 1024 + j * COLS + h * DIM, DIM), DIM)
+
+        def body(s, _):
+            g, jj, tt = peer(s)
+            at = pl.ds(pl.multiple_of(g * ROWS, ROWS), ROWS)
+            to_heads(dq.at[h, at, :], out_ref.at[0, :, cols], jj, tt, dq_send.at[h], dq_recv.at[h]).start()
+            return 0
+
+        lax.fori_loop(1, GROUP, body, 0)
+        pltpu.make_async_copy(dq.at[h, mine, :], out_ref.at[0, :, cols], dq_recv.at[h]).start()
 
     def send_dkv(h):
         cols = pl.ds(pl.multiple_of(t * 1024 + j * COLS + h * DIM, DIM), DIM)
@@ -399,7 +433,7 @@
             sh, sl = split(scores[h, rr, cc])
             d_query = mm(eh, key) + mm(el, key)
             d_query = d_query + use[rr, :] * (mm(hi, th, 1, 1) + mm(hi, tl, 1, 1) + mm(lo, th, 1, 1))
-            dq[rr, pl.ds(pl.multiple_of(h * DIM, DIM), DIM)] = d_query.astype(BF16)
+            dq[h, rr, :] = d_query.astype(BF16)
             d_key = mm(eh, query, 0, 0) + mm(el, query, 0, 0)
             d_value = mm(sh, hi, 0, 0) + mm(sl, hi, 0, 0) + mm(sh, lo, 0, 0)
             if r == 0:
@@ -419,19 +453,6 @@
             device_id=(base + lax.rem(j + s, GZ), t, y), device_id_type=MESH,
         )
 
-    lax.fori_loop(0, HEADS, local_grads, 0)
-    lax.fori_loop(1, GROUP, send_dq, 0)
-    pltpu.make_async_copy(dq.at[mine, :], out_ref.at[0, :, my_cols], dq_recv).start()
-
-    for s in range(1, 4):
-        yy = lax.rem(y + s, 4)
-        pltpu.make_async_copy(gy.at[yy], gy.at[yy], gy_recv.at[yy]).wait()
-    gg[j] = (gy[0] + gy[1]) + (gy[2] + gy[3])
-    for s in range(1, GZ):
-        gg_copy(s).start()
-
-    lax.fori_loop(0, HEADS, backward, 0)
-
     even = lax.rem(p, 2) == 0
     near = jnp.where(even, after, before)
     other = jnp.where(even, before, after)
@@ -443,8 +464,20 @@
         )
 
     def last_grads(h, _):
-        backward_rest(h, 0)
-        gh, gl = split(decode(bm[h]) + far_out * decode(bp[h]))
+        local_grads(h, 0)
+        send_dq(h)
+
+        @pl.when(h == 0)
+        def _():
+            for s in range(1, 4):
+                yy = lax.rem(y + s, 4)
+                pltpu.make_async_copy(gy.at[yy], gy.at[yy], gy_recv.at[yy]).wait()
+            gg[j] = (gy[0] + gy[1]) + (gy[2] + gy[3])
+            for s in range(1, GZ):
+                gg_copy(s).start()
+
+        backward(h, 0)
+        gh, gl = split(decode(b1[h]) + out2 * decode(b2[h]) + out3 * decode(b3[h]))
         key, value = take(0, h), take(1, h)
         d_key = dkl[h] + keep[...] * (mm(value, gh, 1, 1) + mm(value, gl, 1, 1))
         d_value = dvl[h] + keep[...] * (mm(key, gh) + mm(key, gl))
@@ -469,15 +502,18 @@
     gz_copy(1, other).wait_recv()
     gout_ref[...] = (gz[2] + gz[3]) / math.sqrt(4 * SEQ * 128)
 
-    pltpu.make_async_copy(out_ref.at[0], out_ref.at[0], dq_recv).wait()
+    half = pl.ds(0, 4096)
     for h in range(HEADS):
+        part = out_ref.at[0, :, half]
+        pltpu.make_async_copy(part, part, dq_recv.at[h]).wait()
         pltpu.make_async_copy(out_ref.at[1 + h], out_ref.at[1 + h], dkv_recv.at[h]).wait()
     most = pl.ds(0, TOK - ROWS)
-    pltpu.make_async_copy(kv.at[:, most, :], kv.at[:, most, :], kv_send).wait()
-    pltpu.make_async_copy(dq.at[most, :], dq.at[most, :], dq_send).wait()
     for h in range(HEADS):
-        pltpu.make_async_copy(qc.at[h, :, most, :], qc.at[h, :, most, :], qc_send.at[h]).wait()
-        pltpu.make_async_copy(dkv.at[h, :, most, :], dkv.at[h, :, most, :], dkv_send.at[h]).wait()
+        for ref, sem in ((kv, kv_send), (qc, qc_send), (dkv, dkv_send)):
+            part = ref.at[h, :, most, :]
+            pltpu.make_async_copy(part, part, sem.at[h]).wait()
+        part = dq.at[h, most, :]
+        pltpu.make_async_copy(part, part, dq_send.at[h]).wait()
     gz_copy(0, near).wait_send()
     gz_copy(1, other).wait_send()
     for s in range(1, GZ):
@@ -493,11 +529,18 @@
         @pl.when((p == 0) | (p == 3))
         def _():
             minus(own_c, c).wait_send()
-            bplus(sg_c, c).wait_send()
+
+        @pl.when(p == 3)
+        def _():
+            back3(c).wait_send()
+
+        @pl.when(p >= 2)
+        def _():
+            back2(c).wait_send()
 
         @pl.when(p >= 1)
         def _():
-            bminus(sg_c, c).wait_send()
+            back1(c).wait_send()
 
         return 0
 
@@ -530,33 +573,35 @@
             jax.ShapeDtypeStruct((3, ROWS, 8192), BF16),
             jax.ShapeDtypeStruct((8, DIM), F32),
         ),
-        in_specs=[hbm] * 4 + [vmem, smem],
+        in_specs=[hbm] * 6,
         out_specs=(anywhere, vmem),
         scratch_shapes=[
             pltpu.VMEM((4, ROWS, 8192), BF16),
-            pltpu.VMEM((2, TOK, COLS), BF16),
+            pltpu.VMEM((HEADS, 2, TOK, DIM), BF16),
             pltpu.VMEM((HEADS, 2, TOK, DIM), BF16),
             pltpu.VMEM((TOK, TOK), F32),
             pltpu.VMEM((TOK, DIM), F32),
             pltpu.VMEM((TOK, DIM), F32),
-            state, coded, coded, coded, coded, state, state, coded, coded, coded, coded,
+            state, coded, coded, coded, coded, state, coded, coded, coded, coded,
+            pltpu.VMEM((HEADS, TOK, DIM), F32),
             pltpu.VMEM((HEADS, TOK, TOK), F32),
             pltpu.VMEM((HEADS, TOK, DIM), BF16),
             pltpu.VMEM((HEADS, TOK, DIM), BF16),
             pltpu.VMEM((HEADS, TOK, DIM), F32),
             pltpu.VMEM((HEADS, TOK, DIM), F32),
-            pltpu.VMEM((TOK, COLS), BF16),
+            pltpu.VMEM((HEADS, TOK, DIM), BF16),
             pltpu.VMEM((HEADS, 2, TOK, DIM), BF16),
             pltpu.VMEM((8, DIM), F32),
             pltpu.VMEM((4, 8, DIM), F32),
             pltpu.VMEM((GZ, 8, DIM), F32),
             pltpu.VMEM((4, 8, DIM), F32),
-            dma((4,)), dma, dma, dma((HEADS,)), dma((HEADS,)),
+            dma((4,)), dma((HEADS,)), dma((HEADS,)), dma((HEADS,)), dma((HEADS,)),
+            dma((HEADS,)), dma((HEADS,)), dma((HEADS,)), dma((HEADS,)), dma((HEADS,)),
+            dma((HEADS,)), dma((HEADS,)), dma((HEADS,)), dma((HEADS,)), dma((HEADS,)),
             dma((HEADS,)), dma((HEADS,)), dma((HEADS,)), dma((HEADS,)),
-            dma((HEADS,)), dma((HEADS,)), dma((HEADS,)), dma((HEADS,)),
-            dma, dma, dma((HEADS,)), dma((HEADS,)),
             dma((4,)), dma((4,)), dma((GZ,)), dma((GZ,)), dma((2,)), dma((2,)),
             pltpu.SemaphoreType.REGULAR((2,)), pltpu.SemaphoreType.REGULAR((4,)),
+            pltpu.VMEM((8, DIM), F32), pltpu.SMEM((1, 8), jnp.int32), dma((2,)),
         ],
         compiler_params=pltpu.CompilerParams(
             collective_id=1, has_side_effects=True, vmem_limit_bytes=60 * 1024 * 1024

time: 80.5 us -> 76.9 us (0.955)
  the two profiles are of different devices: /device:TPU:1 before, /device:TPU:54 now
where the time goes in v4:
time: 76.9 us; the launch traced here: 76.8 us
  Pallas kernels  76.1 us (99%)
    pallas_call x1, Pallas kernels, local(): pl.pallas_call(kernel, out_shape=(jax.ShapeDtypeStruct((3, ROWS, 8192), B...  73.5 us
    pallas_call x1, Pallas kernels, local(): pl.pallas_call(place, out_shape=(rows, rows, rows, jax.ShapeDtypeStruct((...  2.63 us

profile of v4, /device:TPU:54, one launch (start us, length us, event | category | flops | bytes accessed | tf_op | source)
XLA Modules:
  0.0 76.8 jit_solution(1087444401333357887)
XLA Ops:
  0.6 73.5 %layer.1 = (bf16[3,16,8192]{2,1,0:T(8,128)(2,1)}, f32[8,128]{1,0:T(8,128)}) custom-call(bf16[1,16,8192]{2,1,0:T(8,128)(2,1)} %k_ref.1, bf16[1,16,8192]{2,1,0:T(8,128)(2,1)} %v_ref.1, bf16[1,16,8192]{2,1,0:T(8,128)(2,1)} %q_ref.1, bf16[1,16,8192]{2,1,0:T(8,128)(2,1)} %c_ref.1, f32[8,128]{1,0:T(8,128)} %bitcast.2, s32[1,8]{1,0:T(1,128)} %starts_in.1), custom_call_target="tpu_custom_call" | custom-call | tf_op jit(solution)/shard_map/layer/pallas_call | solution.py:570
  74.1 2.6 %place.1 = (bf16[1,16,8192]{2,1,0:T(8,128)(2,1)}, bf16[1,16,8192]{2,1,0:T(8,128)(2,1)}, bf16[1,16,8192]{2,1,0:T(8,128)(2,1)}, f32[8,128]{1,0:T(8,128)}) custom-call(bf16[3,16,8192]{2,1,0:T(8,128)(2,1)} %get-tuple-element.10.grads_ref, f32[8,128]{1,0:T(8,128)} %get-tuple-element.11.gain_ref), custom_call_target="tpu_custom_call" | custom-call | tf_op jit(solution)/shard_map/place/pallas_call | solution.py:612

commit v5 on v4

--- a/solution.py
+++ b/solution.py
@@ -107,13 +107,10 @@
     def answer(sem, zz, yy):
         pl.semaphore_signal(sem, inc=1, device_id=(zz, t, yy), device_id_type=MESH)
 
-    @pl.when(p > 0)
-    def _():
-        answer(ready.at[0], before, y)
-
-    @pl.when(p == POS - 1)
-    def _():
-        answer(ready.at[1], after, y)
+    for d in range(1, POS):
+        @pl.when(p - d >= 0)
+        def _():
+            answer(ready.at[d - 1], lax.rem(z + SEQ - d * GZ, SEQ), y)
 
     for yy in range(3):
         @pl.when(yy < y)
@@ -343,7 +340,7 @@
 
         @pl.when((h == 0) & (p == 0))
         def _():
-            pl.semaphore_wait(ready.at[1], 1)
+            pl.semaphore_wait(ready.at[2], 1)
 
         forward(h, 0)
 
@@ -453,14 +450,10 @@
             device_id=(base + lax.rem(j + s, GZ), t, y), device_id_type=MESH,
         )
 
-    even = lax.rem(p, 2) == 0
-    near = jnp.where(even, after, before)
-    other = jnp.where(even, before, after)
-
-    def gz_copy(i, partner):
+    def gz_copy(d):
         return pltpu.make_async_remote_copy(
-            src_ref=gz.at[2 * i], dst_ref=gz.at[2 * i + 1], send_sem=gz_send.at[i], recv_sem=gz_recv.at[i],
-            device_id=(partner, t, y), device_id_type=MESH,
+            src_ref=gz.at[p], dst_ref=gz.at[p], send_sem=gz_send.at[d - 1], recv_sem=gz_recv.at[d - 1],
+            device_id=(lax.rem(z + d * GZ, SEQ), t, y), device_id_type=MESH,
         )
 
     def last_grads(h, _):
@@ -490,17 +483,21 @@
             for s in range(1, GZ):
                 jj = lax.rem(j + s, GZ)
                 pltpu.make_async_copy(gg.at[jj], gg.at[jj], gg_recv.at[jj]).wait()
-            gz[0] = (gg[0] + gg[1]) + (gg[2] + gg[3])
-            gz_copy(0, near).start()
+            gz[p] = (gg[0] + gg[1]) + (gg[2] + gg[3])
+
+            @pl.when(p <= 1)
+            def _():
+                pl.semaphore_wait(ready.at[1], 1)
+
+            for d in range(1, POS):
+                gz_copy(d).start()
 
         return 0
 
     lax.fori_loop(0, HEADS, last_grads, 0)
-    gz_copy(0, near).wait_recv()
-    gz[2] = gz[0] + gz[1]
-    gz_copy(1, other).start()
-    gz_copy(1, other).wait_recv()
-    gout_ref[...] = (gz[2] + gz[3]) / math.sqrt(4 * SEQ * 128)
+    for d in range(1, POS):
+        gz_copy(d).wait_recv()
+    gout_ref[...] = ((gz[0] + gz[1]) + (gz[2] + gz[3])) / math.sqrt(4 * SEQ * 128)
 
     half = pl.ds(0, 4096)
     for h in range(HEADS):
@@ -514,8 +511,8 @@
             pltpu.make_async_copy(part, part, sem.at[h]).wait()
         part = dq.at[h, most, :]
         pltpu.make_async_copy(part, part, dq_send.at[h]).wait()
-    gz_copy(0, near).wait_send()
-    gz_copy(1, other).wait_send()
+    for d in range(1, POS):
+        gz_copy(d).wait_send()
     for s in range(1, GZ):
         gg_copy(s).wait_send()
     for s in range(1, 4):
@@ -599,8 +596,8 @@
             dma((HEADS,)), dma((HEADS,)), dma((HEADS,)), dma((HEADS,)), dma((HEADS,)),
             dma((HEADS,)), dma((HEADS,)), dma((HEADS,)), dma((HEADS,)), dma((HEADS,)),
             dma((HEADS,)), dma((HEADS,)), dma((HEADS,)), dma((HEADS,)),
-            dma((4,)), dma((4,)), dma((GZ,)), dma((GZ,)), dma((2,)), dma((2,)),
-            pltpu.SemaphoreType.REGULAR((2,)), pltpu.SemaphoreType.REGULAR((4,)),
+            dma((4,)), dma((4,)), dma((GZ,)), dma((GZ,)), dma((POS - 1,)), dma((POS - 1,)),
+            pltpu.SemaphoreType.REGULAR((3,)), pltpu.SemaphoreType.REGULAR((4,)),
             pltpu.VMEM((8, DIM), F32), pltpu.SMEM((1, 8), jnp.int32), dma((2,)),
         ],
         compiler_params=pltpu.CompilerParams(

time: 76.9 us -> 75.2 us (0.978)
  the two profiles are of different devices: /device:TPU:54 before, /device:TPU:1 now
where the time goes in v5:
time: 75.2 us; the launch traced here: 75 us
  Pallas kernels  74.4 us (99%)
    pallas_call x1, Pallas kernels, local(): pl.pallas_call(kernel, out_shape=(jax.ShapeDtypeStruct((3, ROWS, 8192), B...  71.7 us
    pallas_call x1, Pallas kernels, local(): pl.pallas_call(place, out_shape=(rows, rows, rows, jax.ShapeDtypeStruct((...  2.63 us

profile of v5, /device:TPU:1, one launch (start us, length us, event | category | flops | bytes accessed | tf_op | source)
XLA Modules:
  0.0 75.0 jit_solution(13607331965343898893)
XLA Ops:
  0.6 71.7 %layer.1 = (bf16[3,16,8192]{2,1,0:T(8,128)(2,1)}, f32[8,128]{1,0:T(8,128)}) custom-call(bf16[1,16,8192]{2,1,0:T(8,128)(2,1)} %k_ref.1, bf16[1,16,8192]{2,1,0:T(8,128)(2,1)} %v_ref.1, bf16[1,16,8192]{2,1,0:T(8,128)(2,1)} %q_ref.1, bf16[1,16,8192]{2,1,0:T(8,128)(2,1)} %c_ref.1, f32[8,128]{1,0:T(8,128)} %bitcast.2, s32[1,8]{1,0:T(1,128)} %starts_in.1), custom_call_target="tpu_custom_call" | custom-call | tf_op jit(solution)/shard_map/layer/pallas_call | solution.py:567
  72.4 2.6 %place.1 = (bf16[1,16,8192]{2,1,0:T(8,128)(2,1)}, bf16[1,16,8192]{2,1,0:T(8,128)(2,1)}, bf16[1,16,8192]{2,1,0:T(8,128)(2,1)}, f32[8,128]{1,0:T(8,128)}) custom-call(bf16[3,16,8192]{2,1,0:T(8,128)(2,1)} %get-tuple-element.10.grads_ref, f32[8,128]{1,0:T(8,128)} %get-tuple-element.11.gain_ref), custom_call_target="tpu_custom_call" | custom-call | tf_op jit(solution)/shard_map/place/pallas_call | solution.py:609
